TPU v7x, 32 devices: a whole 2x2x4 slice. The times are simulated.
32 devices in a mesh: dp: 4 (over y, x), expert: 8 (over z, core).
Axes of the slice: x: 2, y: 2, z: 4, core: 2. Of those that a mesh axis runs over, the one named last changes fastest.
Arguments:
- tokens: bfloat16 [64, 6144], P('dp'), may hold values from -6 to 6
- w_gate: bfloat16 [6144, 32768], P(None, ('expert', 'dp')), may hold values from -0.078125 to 0.078125
- w_up: bfloat16 [6144, 32768], P(None, ('expert', 'dp')), may hold values from -0.078125 to 0.078125
- basis: bfloat16 [2, 32768, 6144], P(None, ('expert', 'dp')), may hold values from -5 to 5
- routes: int32 [64, 2], replicated, may hold values from 0 to 3, all different within a row; in each aligned block of 16 rows (0 to 15, 16 to 31, ...) at most 9 rows name the same one
- gates: float32 [64, 2], replicated, may hold values from 0.1 to 0.9
- rho: float32 [64], P('dp'), may hold values from 0.3 to 3
- sigma: float32 [6144], replicated, may hold values from 0.3 to 3
Outputs:
- krylov_next: bfloat16 [32768, 6144], P(('expert', 'dp'))
- hessenberg: float32 [3, 1], replicated
Inputs may be any that keep to these rules, and one draw needn't show every extreme that they name: `routes`: in each aligned block of 16 rows (the rows of one index of dp), no expert is named by more than 9 rows; the 2 entries of a row differ.
All inputs are finite; a program needn't handle non-finite values.
Results may differ from a plain program's by a relative error of at most 0.0062.
The roundings to bfloat16 on the way count: a program that leaves them out, or rounds other values in their place, can miss the bound.
Values may be sent and summed in bfloat16 or wider, within the bound.
No kernel may reach another device: no remote copies, remote signals or barrier semaphores. Data moves between devices by JAX's collectives and lax.ppermute only.
A program may use at most 192 MiB of HBM per device.

v0:
```python
import math

import jax
import jax.numpy as jnp
from jax import lax
from jax.sharding import PartitionSpec as P

FF = 8192
E = 4
BASIS = 2
STEPS = 1
CAP = 9


def slot_tables(routes, gates, expert_id, sources, tok_dev, capacity):
    matches = (routes == expert_id).reshape(sources, tok_dev, routes.shape[1])
    member = jnp.sum(matches.astype(jnp.int32), axis=2)
    gate_tok = jnp.sum(
        jnp.where(matches, gates.reshape(sources, tok_dev, routes.shape[1]), 0.0), axis=2
    )
    slot_rank = jnp.cumsum(member, axis=1) - 1
    slot_index = lax.broadcasted_iota(jnp.int32, (sources, capacity, tok_dev), 1)
    placing = jnp.where(
        (slot_rank[:, None, :] == slot_index) & (member[:, None, :] > 0), 1.0, 0.0
    ).astype(jnp.float32)
    slot_gate = jnp.sum(placing * gate_tok[:, None, :], axis=2)
    return (placing, slot_gate)


def body(tokens, w_gate, w_up, basis, routes, gates, rho, sigma):
    sources = lax.axis_size("dp")
    slices = lax.axis_size("expert") // E
    expert_id = lax.axis_index("expert") // slices
    source = lax.axis_index("dp")
    tok_dev = tokens.shape[0]
    features = tokens.shape[1]
    scale_back = 1.0 / math.sqrt(FF)
    kappa = E * FF / (tok_dev * sources)
    entries = float(E * FF * features)
    placing, slot_gate = slot_tables(routes, gates, expert_id, sources, tok_dev, CAP)
    own_place = lax.dynamic_index_in_dim(placing, source, 0, keepdims=False)
    own_bf = own_place.astype(jnp.bfloat16)
    flat_gate = slot_gate.reshape(-1)
    picked = jnp.dot(own_bf, tokens, preferred_element_type=jnp.float32).astype(jnp.bfloat16)
    piece = lax.all_gather(picked, "dp", axis=0, tiled=True)
    gate_part = jnp.dot(piece, w_gate, preferred_element_type=jnp.float32)
    up_part = jnp.dot(piece, w_up, preferred_element_type=jnp.float32)
    hidden = (jax.nn.silu(gate_part) * up_part * flat_gate[:, None]).astype(jnp.bfloat16)
    current = basis[BASIS - 1]
    direction = current
    row_block = hidden
    own_rows = lax.psum_scatter(
        jnp.dot(row_block, direction, preferred_element_type=jnp.float32) * scale_back,
        "dp",
        scatter_dimension=0,
        tiled=True,
    )
    partial_tok = jnp.dot(own_place.T, own_rows, precision=lax.Precision.HIGHEST)
    response = lax.psum(partial_tok, "expert")
    cotangent = (kappa * rho[:, None] * sigma[None, :] * response).astype(jnp.bfloat16)
    own_cot = jnp.dot(own_bf, cotangent, preferred_element_type=jnp.float32).astype(jnp.bfloat16)
    row_block = hidden
    grad = jnp.dot(
        row_block.T,
        lax.all_gather(own_cot, "dp", axis=0, tiled=True),
        preferred_element_type=jnp.float32,
    )
    image = grad * scale_back
    widened = basis.astype(jnp.float32)
    local_dots = jnp.einsum("bfd,fd->b", widened, image, precision=lax.Precision.HIGHEST)
    coeffs = lax.psum(local_dots, ("dp", "expert")) / entries
    resid = image - jnp.einsum("b,bfd->fd", coeffs, widened, precision=lax.Precision.HIGHEST)
    norm_sq = lax.psum(jnp.sum(resid * resid), ("dp", "expert")) / entries
    beta = jnp.sqrt(norm_sq)
    current, coeffs, beta = ((resid / beta).astype(jnp.bfloat16), coeffs, beta)
    padding = jnp.zeros((STEPS - 1,), jnp.float32)
    columns = [jnp.concatenate([coeffs, padding, beta[None]])]
    return (current, jnp.stack(columns, axis=1))


def solution(mesh):
    return jax.shard_map(
        body,
        mesh=mesh,
        in_specs=(
            P("dp", None),
            P(None, ("expert", "dp")),
            P(None, ("expert", "dp")),
            P(None, ("expert", "dp"), None),
            P(),
            P(),
            P("dp"),
            P(),
        ),
        out_specs=(P(("expert", "dp"), None), P()),
        check_vma=False,
    )
```

profile of v0, /device:TPU:0, one launch (start us, length us, event | category | flops | bytes accessed | tf_op | source)
XLA Modules:
  0.0 477.9 jit_solution(12030863626315866091)
XLA Ops:
  7.2 0.0 copy-start
  7.2 0.0 all-reduce.6.cloned.1.call-start
  7.2 0.7 convert_reduce_fusion
  8.0 0.1 reduce_window_sum.13
  8.1 0.2 reduce_window_sum.14
  8.3 0.7 select_reduce_fusion
  9.0 0.1 mul.64
  9.1 0.1 multiply_reduce_fusion.2
  9.2 0.1 copy.10
  9.2 0.1 mul.67
  9.3 0.0 copy-done
  9.4 0.2 fusion.8
  9.6 12.7 %all-gather = bf16[4,9,6144]{2,1,0:T(8,128)(2,1)S(1)} all-gather(bf16[1,9,6144]{2,1,0:T(8,128)(2,1)S(1)} %fusion.8), channel_id=1, replica_groups=mesh['dp'=4,'expert'=8] {'dp'}, dimensions={0}, use_global_device_ids=true | all-gather | bytes 552960 | tf_op jit(solution)/shard_map/all_gather | solution.py:45
  22.2 0.2 reshape.30
  22.4 0.0 copy-start.3
  22.4 0.0 copy-start.6
  22.4 0.0 copy-start.5
  22.4 0.0 copy-start.4
  22.4 7.0 %fusion.22 = f32[36,1024]{1,0:T(8,128)S(1)} fusion(bf16[36,6144]{1,0:T(8,128)(2,1)S(1)} %reshape.30, bf16[6144,1024]{1,0:T(8,128)(2,1)} %param.9), kind=kOutput, calls=%fused_computation.41 | convolution fusion | flops 452984832 | bytes 13172736 | tf_op jit(solution)/shard_map/dot_general | solution.py:46
  29.4 7.7 %fusion.11 = bf16[36,1024]{1,0:T(8,128)(2,1)S(1)} fusion(bf16[36,6144]{1,0:T(8,128)(2,1)S(1)} %reshape.30, bf16[6144,1024]{1,0:T(8,128)(2,1)} %param.10, f32[36,1024]{1,0:T(8,128)S(1)} %fusion.22, f32[36]{0:T(128)S(1)} %mul.67), kind=kOutput, calls=%fused_computation.17 | convolution fusion | flops 453242880 | bytes 13246608 | tf_op jit(solution)/shard_map/dot_general | solution.py:47
  37.1 0.6 copy-done.3
  37.7 3.2 fusion.5
  40.9 0.0 all-reduce.6.cloned.1.call-update
  41.0 0.0 all-reduce.4.cloned.1.call-start
  41.0 0.0 copy-done.6
  41.0 0.6 dynamic-slice
  42.3 50.7 %all-reduce.6.cloned.1.call-done = f32[36,6144]{1,0:T(8,128)} async-done(((f32[36,6144]{1,0:T(8,128)}), f32[36,6144]{1,0:T(8,128)}) %all-reduce.6.cloned.1.call-update) | async-done | bytes 884752
  93.0 2.3 fusion.12
  95.3 0.0 all-reduce.4.cloned.1.call-update
  95.3 0.0 copy-done.5
  95.4 56.0 %all-reduce.4.cloned.1.call-done = f32[16,6144]{1,0:T(8,128)} async-done(((f32[16,6144]{1,0:T(8,128)}), f32[16,6144]{1,0:T(8,128)}) %all-reduce.4.cloned.1.call-update) | async-done | bytes 393232 | tf_op jit(solution)/shard_map/psum | solution.py:59
  151.3 0.0 copy-done.4
  151.3 1.2 fusion.9
  152.6 11.9 %all-gather.1 = bf16[4,9,6144]{2,1,0:T(8,128)(2,1)S(1)} all-gather(bf16[1,9,6144]{2,1,0:T(8,128)(2,1)S(1)} %fusion.9), channel_id=1, replica_groups=mesh['dp'=4,'expert'=8] {'dp'}, dimensions={0}, use_global_device_ids=true | all-gather | bytes 552960 | tf_op jit(solution)/shard_map/all_gather | solution.py:65
  164.4 0.2 reshape.32
  164.6 3.5 fusion.23
  168.1 0.0 copy-start.2
  168.1 8.3 %copy-done.2 = f32[1024,6144]{1,0:T(8,128)} copy-done((f32[1024,6144]{1,0:T(8,128)}, f32[1024,6144]{1,0:T(8,128)S(1)}, u32[]{:S(2)}) %copy-start.2) | copy-done | bytes 25165848
  176.4 8.7 %multiply_bitcast_fusion = f32[6144,1024]{0,1:T(8,128)} fusion(f32[1024,6144]{1,0:T(8,128)S(1)} %fusion.23), kind=kLoop, calls=%fused_computation.6 | loop fusion | flops 6291456 | bytes 50331648
  185.1 19.6 %multiply_reduce_fusion = f32[2]{0:T(128)S(1)} fusion(f32[6144,1024]{0,1:T(8,128)} %multiply_bitcast_fusion, bf16[2,1024,6144]{2,1,0:T(8,128)(2,1)} %param.11), kind=kLoop, calls=%fused_computation | loop fusion | flops 37748736 | bytes 50331656 | tf_op jit(solution)/shard_map/bfd,fd->b/dot_general | solution.py:70
  204.7 38.7 %psum.22 = f32[2]{0:T(128)S(1)} all-reduce(f32[2]{0:T(128)S(1)} %multiply_reduce_fusion), channel_id=1, replica_groups=mesh['dp'=4,'expert'=8] {'dp','expert'}, use_global_device_ids=true, to_apply=%region_6.7 | all-reduce | flops 2 | bytes 16 | tf_op jit(solution)/shard_map/psum | solution.py:71
  243.4 139.7 %fusion = f32[1,1024,6144]{2,0,1:T(1,128)} fusion(bf16[2,1024,6144]{2,1,0:T(8,128)(2,1)} %param.11, f32[2]{0:T(128)S(1)} %psum.22), kind=kOutput, calls=%fused_computation.4 | convolution fusion | flops 150994944 | bytes 50331656 | tf_op jit(solution)/shard_map/b,bfd->fd/dot_general | solution.py:72
  383.2 21.0 %multiply_reduce_fusion.1 = f32[]{:T(128)} fusion(f32[1,1024,6144]{2,0,1:T(1,128)} %fusion, f32[1024,6144]{1,0:T(8,128)} %copy-done.2), kind=kLoop, calls=%fused_computation.3 | loop fusion | flops 25165824 | bytes 50331652 | tf_op jit(solution)/shard_map/reduce_sum | solution.py:73
  404.2 41.3 %psum.23 = f32[]{:T(128)} all-reduce(f32[]{:T(128)} %multiply_reduce_fusion.1), channel_id=1, replica_groups=mesh['dp'=4,'expert'=8] {'dp','expert'}, use_global_device_ids=true, to_apply=%region_8.9 | all-reduce | flops 1 | bytes 8 | tf_op jit(solution)/shard_map/psum | solution.py:73
  446.2 0.0 copy-start.1
  446.2 24.2 %divide_convert_fusion = bf16[1024,6144]{1,0:T(8,128)(2,1)} fusion(f32[]{:T(128)} %sqrt.3, f32[1,1024,6144]{2,0,1:T(1,128)} %fusion, f32[1024,6144]{1,0:T(8,128)} %copy-done.2), kind=kLoop, calls=%fused_computation.2 | loop fusion | flops 25165824 | bytes 62914564 | tf_op jit(solution)/shard_map/convert_element_type | solution.py:75
  470.4 0.6 maximum_bitcast_fusion
  471.0 0.0 copy-done.1
  (5 shorter events, 0.0 us)
Async XLA Ops:
  7.2 2.2 copy-start
  7.2 85.8 %all-reduce.6.cloned.1.call-start = ((), (), s32[]{:S(2)}) async-start(), calls=%async_computation.1 | async-start | bytes 1966080
  22.4 15.3 %copy-start.3 = (bf16[2,1024,6144]{2,1,0:T(8,128)(2,1)S(1)}, bf16[2,1024,6144]{2,1,0:T(8,128)(2,1)}, u32[]{:S(2)}) copy-start(bf16[2,1024,6144]{2,1,0:T(8,128)(2,1)} %param.11) | copy-start | bytes 75497472
  22.4 18.6 %copy-start.6 = (u32[32]{0:T(128)S(1)}, u32[32]{0:T(128)}, u32[]{:S(2)}) copy-start(u32[32]{0:T(128)} %constant.53) | copy-start | bytes 388
  22.4 72.9 %copy-start.5 = (f32[16]{0:T(128)S(1)}, f32[16]{0:T(128)}, u32[]{:S(2)}) copy-start(f32[16]{0:T(128)} %param.14) | copy-start | bytes 196
  22.4 128.9 %copy-start.4 = (f32[6144]{0:T(1024)S(1)}, f32[6144]{0:T(1024)}, u32[]{:S(2)}) copy-start(f32[6144]{0:T(1024)} %param.15) | copy-start | bytes 73732
  41.0 110.4 %all-reduce.4.cloned.1.call-start = ((), (), s32[]{:S(2)}) async-start(), calls=%async_computation | async-start | bytes 786432 | tf_op jit(solution)/shard_map/psum | solution.py:59
  168.1 8.3 %copy-start.2 = (f32[1024,6144]{1,0:T(8,128)}, f32[1024,6144]{1,0:T(8,128)S(1)}, u32[]{:S(2)}) copy-start(f32[1024,6144]{1,0:T(8,128)S(1)} %fusion.23) | copy-start | bytes 75497472
  446.2 24.9 %copy-start.1 = (bf16[16,6144]{1,0:T(8,128)(2,1)S(1)}, bf16[16,6144]{1,0:T(8,128)(2,1)}, u32[]{:S(2)}) copy-start(bf16[16,6144]{1,0:T(8,128)(2,1)} %param.8) | copy-start | bytes 589828
Sparse Core Ops, SparseCore 0:
  41.1 51.8 all-reduce.5
  95.9 55.4 all-reduce.3
where the time goes:
time: 478 us
  matrix products  165 us (35%)
  waiting for transfers between devices  107 us (22%)
  blocking collectives  105 us (22%)
  other arithmetic  75.9 us (16%)
  between operations  15.6 us (3%)
  local copies, waits for them, and re-layouts  10.2 us (2%)
    dot_general x1, matrix products, body(): jnp.einsum('b,bfd->fd', coeffs, widened, precision=lax.Precision.HIGHEST)  140 us
    psum x1, waiting for transfers between devices, body(): response = lax.psum(partial_tok, 'expert')  56 us
    unnamed x3, waiting for transfers between devices  50.7 us
    psum x1, blocking collectives, body(): norm_sq = lax.psum(jnp.sum(resid * resid), ('dp', 'expert')) / entries  41.3 us
    psum x1, blocking collectives, body(): coeffs = lax.psum(local_dots, ('dp', 'expert')) / entries  38.7 us
    convert_element_type x1, other arithmetic, body(): current, coeffs, beta = ((resid / beta).astype(jnp.bfloat16), coeffs, beta)  24.2 us
    reduce_sum x1, other arithmetic, body(): norm_sq = lax.psum(jnp.sum(resid * resid), ('dp', 'expert')) / entries  21 us
    dot_general x1, other arithmetic, body(): jnp.einsum('bfd,fd->b', widened, image, precision=lax.Precision.HIGHEST)  19.6 us
  transfers between devices with their start and end apart: 2, of which 2 were waited for; matrix products, arithmetic and copies ran while one was open for 0% of the time, Pallas kernels for 0%

commit v1 on v0

v1 whole, which is shorter than its diff:
```python
import functools
import math

import jax
import jax.numpy as jnp
from jax import lax
from jax.experimental import pallas as pl
from jax.experimental.pallas import tpu as pltpu
from jax.sharding import Mesh, PartitionSpec as P

FF = 8192
E = 4
BASIS = 2
STEPS = 1
CAP = 9
MIB = 1 << 20
F32 = jnp.float32
BF16 = jnp.bfloat16
PLANE = ("dp", "slice")
EVERY = ("dp", "group", "slice")


def params(mib=None):
    return pltpu.CompilerParams(vmem_limit_bytes=mib * MIB if mib else None)


def dot(a, b, dims=((1,), (0,))):
    return lax.dot_general(a, b, (dims, ((), ())), preferred_element_type=F32)


def divisor(total, unit, limit):
    best = unit
    for size in range(unit, limit + 1, unit):
        if total % size == 0:
            best = size
    return best


def slot_tables(routes, gates, experts, sources, tok_dev, rows):
    total = sources * tok_dev
    matches = routes[None, :, :] == experts[:, None, None]
    member = jnp.sum(matches.astype(jnp.int32), axis=2)
    gate_tok = jnp.sum(jnp.where(matches, gates[None], 0.0), axis=2)
    token = lax.broadcasted_iota(jnp.int32, (total, total), 0)
    other = lax.broadcasted_iota(jnp.int32, (total, total), 1)
    earlier = (token // tok_dev == other // tok_dev) & (other < token)
    rank = jnp.sum(jnp.where(earlier[None], member[:, None, :], 0), axis=2)
    source = lax.broadcasted_iota(jnp.int32, (1, total), 1) // tok_dev
    slot = jnp.where(member > 0, source * CAP + rank, -1)
    row = lax.broadcasted_iota(jnp.int32, (1, rows, 1), 1)
    placing = (slot[:, None, :] == row).astype(BF16)
    return placing, gate_tok


def hidden_kernel(steps, x_ref, wg_ref, wu_ref, gate_ref, place_ref, out_ref, acc_g, acc_u):
    step = pl.program_id(0)
    x = x_ref[...]
    part_g, part_u = dot(x, wg_ref[...]), dot(x, wu_ref[...])

    @pl.when(step == 0)
    def _():
        acc_g[...] = part_g
        acc_u[...] = part_u

    @pl.when(step > 0)
    def _():
        acc_g[...] += part_g
        acc_u[...] += part_u

    @pl.when(step == steps - 1)
    def _():
        g = acc_g[...]
        full = (g * (1.0 / (1.0 + jnp.exp(-g))) * acc_u[...] * gate_ref[...]).astype(BF16)
        out_ref[...] = dot(place_ref[...], full).astype(BF16)


def hidden_call(x, w_gate, w_up, gate_col, placing):
    tokens, features = x.shape
    units = w_gate.shape[1]
    rows = placing.shape[0]
    depth = divisor(features, 128, 512)
    steps = features // depth
    return pl.pallas_call(
        functools.partial(hidden_kernel, steps),
        grid=(steps,),
        in_specs=[
            pl.BlockSpec((tokens, depth), lambda i: (0, i)),
            pl.BlockSpec((depth, units), lambda i: (i, 0)),
            pl.BlockSpec((depth, units), lambda i: (i, 0)),
            pl.BlockSpec((tokens, 1), lambda i: (0, 0)),
            pl.BlockSpec((rows, tokens), lambda i: (0, 0)),
        ],
        out_specs=pl.BlockSpec((rows, units), lambda i: (0, 0)),
        out_shape=jax.ShapeDtypeStruct((rows, units), BF16),
        scratch_shapes=[pltpu.VMEM((tokens, units), F32)] * 2,
        compiler_params=params(24),
        cost_estimate=pl.CostEstimate(
            flops=4 * tokens * features * units, bytes_accessed=4 * features * units, transcendentals=0
        ),
        name="hidden",
    )(x, w_gate, w_up, gate_col, placing)


def tangent_kernel(scale, place_ref, h_ref, v_ref, out_ref):
    out_ref[0] = (dot(h_ref[...], v_ref[0]) * scale).astype(BF16)


def tangent_call(hidden, basis, index, position, chunks, scale):
    rows, units = hidden.shape
    features = basis.shape[2]
    wide = features // chunks
    return pl.pallas_call(
        functools.partial(tangent_kernel, scale),
        grid_spec=pltpu.PrefetchScalarGridSpec(
            num_scalar_prefetch=1,
            grid=(chunks,),
            in_specs=[
                pl.BlockSpec((rows, units), lambda c, pos: (0, 0)),
                pl.BlockSpec((1, units, wide), lambda c, pos: (index, 0, c)),
            ],
            out_specs=pl.BlockSpec((1, rows, wide), lambda c, pos: (pos[c], 0, 0)),
        ),
        out_shape=jax.ShapeDtypeStruct((chunks, rows, wide), BF16),
        compiler_params=params(16),
        cost_estimate=pl.CostEstimate(
            flops=2 * rows * features * units, bytes_accessed=2 * features * units, transcendentals=0
        ),
        name="tangent",
    )(position, hidden, basis)


def other_kernel(scale, h_ref, v_ref, out_ref, gram_ref, sums):
    step = pl.program_id(0)

    @pl.when(step == 0)
    def _():
        sums[...] = jnp.zeros_like(sums)

    out_ref[0] = (dot(h_ref[...], v_ref[0]) * scale).astype(BF16)
    units = v_ref.shape[1]
    strip = 32 if units % 32 == 0 else units
    wide = v_ref.shape[2]

    def body(i, carry):
        a = v_ref[0, pl.ds(i * strip, strip), :].astype(F32)
        b = v_ref[1, pl.ds(i * strip, strip), :].astype(F32)
        fold = lambda x: jnp.sum(x.reshape(strip // 8, 8, wide), axis=0)
        return carry[0] + fold(a * a), carry[1] + fold(a * b), carry[2] + fold(b * b)

    zero = jnp.zeros((8, wide), F32)
    aa, ab, bb = lax.fori_loop(0, units // strip, body, (zero, zero, zero))
    sums[0] += aa
    sums[1] += ab
    sums[2] += bb

    @pl.when(step == pl.num_programs(0) - 1)
    def _():
        line = lax.broadcasted_iota(jnp.int32, (8, 128), 0)
        gram = jnp.where(line == 3, jnp.sum(sums[0]), 0.0)
        gram = jnp.where(line == 4, jnp.sum(sums[1]), gram)
        gram_ref[...] = jnp.where(line == 5, jnp.sum(sums[2]), gram)


def other_call(hidden, basis, chunks, scale):
    rows, units = hidden.shape
    features = basis.shape[2]
    wide = features // chunks
    return pl.pallas_call(
        functools.partial(other_kernel, scale),
        grid=(chunks,),
        in_specs=[
            pl.BlockSpec((rows, units), lambda c: (0, 0)),
            pl.BlockSpec((BASIS, units, wide), lambda c: (0, 0, c)),
        ],
        out_specs=[
            pl.BlockSpec((1, rows, wide), lambda c: (c, 0, 0)),
            pl.BlockSpec((8, 128), lambda c: (0, 0)),
        ],
        out_shape=[
            jax.ShapeDtypeStruct((chunks, rows, wide), BF16),
            jax.ShapeDtypeStruct((8, 128), F32),
        ],
        scratch_shapes=[pltpu.VMEM((3, 8, wide), F32)],
        compiler_params=params(16),
        cost_estimate=pl.CostEstimate(
            flops=2 * rows * features * units, bytes_accessed=4 * features * units, transcendentals=0
        ),
        name="other_tangent",
    )(hidden, basis)


def pieces(x):
    first = x.astype(BF16)
    rest = x - first.astype(F32)
    second = rest.astype(BF16)
    return first, second, (rest - second.astype(F32)).astype(BF16)


def share_kernel(line, parts, *refs):
    ins, rho_ref, outs = refs[:parts], refs[parts], refs[parts + 1 :]
    rows, wide = ins[0].shape[1:]
    row = lax.broadcasted_iota(jnp.int32, (rows, wide), 0)
    for j, out_ref in enumerate(outs):
        total = ins[0][j].astype(F32)
        for ref in ins[1:]:
            total = total + ref[j].astype(F32)
        if j:
            for n, piece in enumerate(pieces(rho_ref[...])):
                total = jnp.where(row == line + n, piece.astype(F32), total)
        out_ref[...] = total.astype(out_ref.dtype)


def share_call(parts, rho_row, line):
    sources, rows, wide = parts[0].shape
    return pl.pallas_call(
        functools.partial(share_kernel, line, len(parts)),
        out_shape=[jax.ShapeDtypeStruct((rows, wide), BF16 if j else F32) for j in range(sources)],
        compiler_params=params(16),
        name="slice_sum",
    )(*parts, rho_row)


def sum_kernel(line, *refs):
    ins, rho_own, out_ref, rho_ref = refs[:-3], refs[-3], refs[-2], refs[-1]
    total = ins[0][...]
    rho_ref[0:1, :] = rho_own[:, 0:128]
    for j, ref in enumerate(ins[1:]):
        part = ref[...].astype(F32)
        total = total + part
        rho_ref[j + 1 : j + 2, :] = (
            part[line : line + 1, 0:128] + part[line + 1 : line + 2, 0:128] + part[line + 2 : line + 3, 0:128]
        )
    row = lax.broadcasted_iota(jnp.int32, total.shape, 0)
    out_ref[...] = jnp.where(row < line, total, 0.0).astype(BF16)


def sum_call(parts, rho_row, line):
    rows, wide = parts[0].shape
    return pl.pallas_call(
        functools.partial(sum_kernel, line),
        out_shape=[
            jax.ShapeDtypeStruct((rows, wide), BF16),
            jax.ShapeDtypeStruct((len(parts), 128), F32),
        ],
        compiler_params=params(16),
        name="plane_sum",
    )(*parts, rho_row)


def cotangent_kernel(parts, place_ref, rho_ref, sigma_ref, *refs):
    ins, out_ref = refs[:parts], refs[parts]
    response = None
    for j, ref in enumerate(ins):
        term = dot(place_ref[j], ref[...], ((0,), (0,)))
        response = term if response is None else response + term
    cot = (rho_ref[...] * sigma_ref[...] * response).astype(BF16)
    out_ref[...] = dot(place_ref[0], cot).astype(BF16)


def cotangent_call(parts, placing, rho_col, sigma_row):
    return pl.pallas_call(
        functools.partial(cotangent_kernel, len(parts)),
        out_shape=jax.ShapeDtypeStruct(parts[0].shape, BF16),
        compiler_params=params(16),
        name="cotangent",
    )(placing, rho_col, sigma_row, *parts)


def products_kernel(scale, pos_ref, h_ref, c_ref, t0_ref, t1_ref, gram_ref, out_ref):
    chunks, rows, _ = c_ref.shape
    h = h_ref[...]
    weight = dot(h, h, ((1,), (1,)))
    c0 = jnp.zeros(c_ref.shape[1:], F32)
    c1 = jnp.zeros(c_ref.shape[1:], F32)
    square = jnp.zeros((rows, rows), F32)
    for c in range(chunks):
        cot = c_ref[c]
        wide = cot.astype(F32)
        c0 = c0 + wide * t0_ref[c].astype(F32)
        c1 = c1 + wide * t1_ref[pos_ref[c]].astype(F32)
        square = square + dot(cot, cot, ((1,), (1,)))
    line = lax.broadcasted_iota(jnp.int32, (8, 128), 0)
    out = jnp.where(line == 0, jnp.sum(c0), gram_ref[...])
    out = jnp.where(line == 1, jnp.sum(c1), out)
    out_ref[...] = jnp.where(line == 2, jnp.sum(weight * square) * (scale * scale), out)


def products_call(position, hidden, cot, t0, t1, gram, scale):
    vmem = pl.BlockSpec(memory_space=pltpu.VMEM)
    return pl.pallas_call(
        functools.partial(products_kernel, scale),
        in_specs=[pl.BlockSpec(memory_space=pltpu.SMEM)] + [vmem] * 5,
        out_specs=vmem,
        out_shape=jax.ShapeDtypeStruct((8, 128), F32),
        compiler_params=params(16),
        name="products",
    )(position, hidden, cot, t0, t1, gram)


def final_kernel(scale, entries, parts_ref, ht_ref, c_ref, v_ref, out_ref, hess_ref, scalars):
    @pl.when(pl.program_id(0) == 0)
    def _():
        total = jnp.sum(parts_ref[...], axis=0) * (1.0 / entries)
        c0, c1, square = total[0:1], total[1:2], total[2:3]
        g00, g01, g11 = total[3:4], total[4:5], total[5:6]
        norm = square - 2.0 * (c0 * c0 + c1 * c1) + c0 * c0 * g00 + 2.0 * c0 * c1 * g01 + c1 * c1 * g11
        beta = jnp.sqrt(jnp.maximum(norm, square * 2.0**-24))
        line = lax.broadcasted_iota(jnp.int32, (8, 128), 0)
        hess_ref[...] = jnp.where(line == 0, c0, jnp.where(line == 1, c1, beta))
        inverse = 1.0 / beta
        scalars[0] = (c0 * inverse)[0, 0]
        scalars[1] = (c1 * inverse)[0, 0]
        scalars[2] = (scale * inverse)[0, 0]

    a0, a1, s = scalars[0], scalars[1], scalars[2]
    units = ht_ref.shape[0]
    strip = 128 if units % 128 == 0 else units
    cot = c_ref[0]
    for i in range(units // strip):
        at = pl.ds(i * strip, strip)
        image = dot(ht_ref[at, :], cot)
        out = image * s - a0 * v_ref[0, at, :].astype(F32) - a1 * v_ref[1, at, :].astype(F32)
        out_ref[at, :] = out.astype(BF16)


def final_call(parts, hidden_t, cot, basis, scale, entries):
    units, rows = hidden_t.shape
    chunks, _, wide = cot.shape
    return pl.pallas_call(
        functools.partial(final_kernel, scale, entries),
        grid=(chunks,),
        in_specs=[
            pl.BlockSpec(parts.shape, lambda c: (0, 0, 0)),
            pl.BlockSpec((units, rows), lambda c: (0, 0)),
            pl.BlockSpec((1, rows, wide), lambda c: (c, 0, 0)),
            pl.BlockSpec((BASIS, units, wide), lambda c: (0, 0, c)),
        ],
        out_specs=[
            pl.BlockSpec((units, wide), lambda c: (0, c)),
            pl.BlockSpec((8, 128), lambda c: (0, 0)),
        ],
        out_shape=[
            jax.ShapeDtypeStruct((units, chunks * wide), BF16),
            jax.ShapeDtypeStruct((8, 128), F32),
        ],
        scratch_shapes=[pltpu.SMEM((4,), F32)],
        compiler_params=params(32),
        cost_estimate=pl.CostEstimate(
            flops=2 * rows * units * chunks * wide, bytes_accessed=6 * units * chunks * wide, transcendentals=0
        ),
        name="residual",
    )(parts, hidden_t, cot, basis)


def swap(x, axis, distance):
    size = lax.axis_size(axis)
    return lax.ppermute(x, axis, [(i, i ^ distance) for i in range(size)])


def body(tokens, w_gate, w_up, basis, routes, gates, rho, sigma):
    sources, slices = lax.axis_size("dp"), lax.axis_size("slice")
    source, group, part = lax.axis_index("dp"), lax.axis_index("group"), lax.axis_index("slice")
    tok_dev, features = tokens.shape
    total = tok_dev * sources
    scale = 1.0 / math.sqrt(FF)
    kappa = E * FF / total
    entries = float(E * FF * features)
    line = sources * CAP
    rows = -(-(line + 3) // 8) * 8
    split = features % (slices * sources * 128) == 0
    cuts = slices if split else 1
    chunks = sources * cuts
    wide = features // chunks
    column = lax.broadcasted_iota(jnp.int32, (chunks,), 0)
    position = ((column % cuts) ^ (part if split else 0)) * sources + ((column // cuts) ^ source)
    own = source * cuts + (part if split else 0)

    placing, gate_tok = slot_tables(
        routes, gates, group ^ jnp.arange(E, dtype=jnp.int32), sources, tok_dev, rows
    )
    w_gate, w_up, basis = (pltpu.with_memory_space_constraint(x, pltpu.HBM) for x in (w_gate, w_up, basis))
    everyone = lax.all_gather(tokens, "dp", axis=0, tiled=True)
    hidden = hidden_call(everyone, w_gate, w_up, gate_tok[0][:, None], placing[0])

    t1 = tangent_call(hidden, basis, BASIS - 1, position, chunks, scale)
    by_slice = t1.reshape(cuts, sources, rows, wide)
    if split:
        got = [by_slice[0]] + [swap(by_slice[j], "slice", j) for j in range(1, slices)]
    else:
        got = [lax.psum(by_slice[0].astype(F32), "slice")]
    rho_row = jnp.pad(rho[None, :], ((0, 0), (0, wide - tok_dev)))
    shares = share_call(got, rho_row, line)
    got = [shares[0]] + [swap(shares[j], "dp", j) for j in range(1, sources)]
    t0, gram = other_call(hidden, basis, chunks, scale)
    summed, rho_all = sum_call(got, rho_row, line)
    got = [summed] + [swap(summed, "group", j) for j in range(1, E)]
    order = source ^ jnp.arange(sources, dtype=jnp.int32)
    pick = order[:, None] == jnp.arange(sources, dtype=jnp.int32)[None, :]
    rho_all = jnp.sum(jnp.where(pick[:, :, None], rho_all[None, :, :tok_dev], 0.0), axis=1)
    rho_col = (kappa * rho_all).reshape(total, 1)
    sigma_row = lax.dynamic_index_in_dim(sigma.reshape(chunks, wide), own, 0, keepdims=True)
    cot = cotangent_call(got, placing, rho_col, sigma_row)
    cot = lax.all_gather(cot, PLANE if split else "dp", axis=0)

    sums = products_call(position, hidden, cot, t0, t1, gram, scale)
    devices = sources * E * slices
    sums = lax.all_to_all(jnp.broadcast_to(sums, (devices, 8, 128)), EVERY, 0, 0, tiled=True)
    new, hess = final_call(sums, hidden.T, cot, basis, scale, entries)
    return new, hess[: BASIS + 1, :1]


def solution(mesh):
    sources, experts = mesh.shape["dp"], mesh.shape["expert"]
    fine = Mesh(mesh.devices.reshape(sources, E, experts // E), EVERY)
    units = ("group", "slice", "dp")
    return jax.shard_map(
        body,
        mesh=fine,
        in_specs=(
            P("dp", None),
            P(None, units),
            P(None, units),
            P(None, units, None),
            P(),
            P(),
            P("dp"),
            P(),
        ),
        out_specs=(P(units, None), P()),
        check_vma=False,
    )
```

time: 478 us -> 108 us (0.23)
  matrix products: 165 us -> 0 us
  waiting for transfers between devices: 107 us -> 13.5 us
  blocking collectives: 105 us -> 22.5 us
  other arithmetic: 75.9 us -> 1.99 us
  Pallas kernels: 0 us -> 55.1 us
  between operations: 15.6 us -> 0.88 us
  starting transfers between devices: 0.08 us -> 11.9 us
  local copies, waits for them, and re-layouts: 10.2 us -> 1.69 us
    dot_general x8 -> x0, matrix products: 165 us -> none  [the longest x1 140 us: body(): jnp.einsum('b,bfd->fd', coeffs, widened, precision=lax.Precision.HIGHEST)]
    psum x2 -> x0, blocking collectives: 80 us -> none  [the longest x1 41.3 us: body(): norm_sq = lax.psum(jnp.sum(resid * resid), ('dp', 'expert')) / entries]
    psum x1 -> x0, waiting for transfers between devices: 56 us -> none  [body(): response = lax.psum(partial_tok, 'expert')]
    pallas_call x0 -> x8, Pallas kernels: none -> 55.1 us  [the longest x1 16.6 us: final_call(): pl.pallas_call(functools.partial(final_kernel, scale, entries), grid=(chu...]
    unnamed x3 -> x0, waiting for transfers between devices: 50.7 us -> none
    convert_element_type x1, other arithmetic: 24.2 us -> 0.02 us  [slot_tables(): placing = (slot[:, None, :] == row).astype(BF16)]
    reduce_sum x3, other arithmetic: 21.8 us -> 1.01 us  [the longest x1 0.77 us: slot_tables(): gate_tok = jnp.sum(jnp.where(matches, gates[None], 0.0), axis=2)]
    dot_general x1 -> x0, other arithmetic: 19.6 us -> none  [body(): jnp.einsum('bfd,fd->b', widened, image, precision=lax.Precision.HIGHEST)]
  transfers between devices with their start and end apart: 2 -> 8, of which waited for: 2 -> 4; matrix products, arithmetic and copies ran while one was open for 0% -> 0% of each run, Pallas kernels for 0% -> 13%
where the time goes in v1:
time: 108 us
  Pallas kernels  55.1 us (51%)
  blocking collectives  22.5 us (21%)
  waiting for transfers between devices  13.5 us (12%)
  starting transfers between devices  11.9 us (11%)
  other arithmetic  1.99 us (2%)
  local copies, waits for them, and re-layouts  1.69 us (2%)
    pallas_call x1, Pallas kernels, final_call(): pl.pallas_call(functools.partial(final_kernel, scale, entries), grid=(chu...  16.6 us
    pallas_call x1, Pallas kernels, hidden_call(): pl.pallas_call(functools.partial(hidden_kernel, steps), grid=(steps,), in...  14.2 us
    pallas_call x1, Pallas kernels, other_call(): pl.pallas_call(functools.partial(other_kernel, scale), grid=(chunks,), in...  14.1 us
    all_gather x1, blocking collectives, body(): everyone = lax.all_gather(tokens, 'dp', axis=0, tiled=True)  13.8 us
    all_gather x1, blocking collectives, body(): cot = lax.all_gather(cot, PLANE if split else 'dp', axis=0)  8.67 us
    pallas_call x1, Pallas kernels, tangent_call(): pl.pallas_call(functools.partial(tangent_kernel, scale), grid_spec=pltpu....  8.59 us
    ppermute x7, starting transfers between devices, swap(): return lax.ppermute(x, axis, [(i, i ^ distance) for i in range(size)])  8.08 us
    all_to_all x1, waiting for transfers between devices, body(): lax.all_to_all(jnp.broadcast_to(sums, (devices, 8, 128)), EVERY, 0, 0, ti...  8 us
  transfers between devices with their start and end apart: 8, of which 4 were waited for; matrix products, arithmetic and copies ran while one was open for 0% of the time, Pallas kernels for 13%

profile of v1, /device:TPU:0, one launch (start us, length us, event | category | flops | bytes accessed | tf_op | source)
XLA Modules:
  0.0 107.6 jit_solution(17466516614215365749)
XLA Ops:
  0.7 0.8 fusion.3
  1.4 0.8 fusion.2
  2.2 0.1 copy.16.gate_ref
  2.3 0.1 fusion.1
  2.4 0.1 select_reduce_fusion
  2.6 13.8 %all_gather.9.x_ref = bf16[64,6144]{1,0:T(8,128)(2,1)S(1)} all-gather(bf16[16,6144]{1,0:T(8,128)(2,1)} %param.8), channel_id=1, replica_groups=mesh['dp'=4,'group'=4,'slice'=2] {'dp'}, dimensions={0}, use_global_device_ids=true | all-gather | bytes 983040 | tf_op jit(solution)/shard_map/all_gather | solution.py:382
  16.4 14.2 %hidden.1.h_ref = bf16[40,1024]{1,0:T(8,128)(2,1)S(1)} custom-call(bf16[64,6144]{1,0:T(8,128)(2,1)S(1)} %all_gather.9.x_ref, bf16[6144,1024]{1,0:T(8,128)(2,1)} %wg_ref.1, bf16[6144,1024]{1,0:T(8,128)(2,1)} %wu_ref.1, f32[64,1]{1,0:T(8,128)S(1)} %copy.16.gate_ref, bf16[40,64]{1,0:T(8,128)(2,1)S(1)} %slice_bitcast_fusion.place_ref), custom_call_target="tpu_custom_call" | custom-call | flops 1610612736 | bytes 25165824 | tf_op jit(solution)/shard_map/hidden/pallas_call | solution.py:83
  30.6 0.0 copy-start
  30.6 0.0 copy-start.1
  30.6 8.6 %tangent.1.t1_ref = bf16[8,40,768]{2,1,0:T(8,128)(2,1)S(1)} custom-call(s32[8]{0:T(128)S(1)} %fusion.6.place_ref.pos_ref, bf16[40,1024]{1,0:T(8,128)(2,1)S(1)} %hidden.1.h_ref, bf16[2,1024,6144]{2,1,0:T(8,128)(2,1)} %v_ref.5), custom_call_target="tpu_custom_call" | custom-call | flops 503316480 | bytes 12582912 | tf_op jit(solution)/shard_map/tangent/pallas_call | solution.py:112
  39.3 0.1 collective-permute-start
  39.4 0.0 copy-done
  39.4 0.0 copy-done.1
  39.4 0.1 iota_compare_fusion.2
  39.5 1.4 %collective-permute-done.refs_1_ = bf16[4,40,768]{2,1,0:T(8,128)(2,1)S(1)} collective-permute-done((bf16[4,40,768]{2,1,0:T(8,128)(2,1)S(1)}, bf16[4,40,768]{2,1,0:T(8,128)(2,1)S(1)}, u32[]{:S(2)}, u32[]{:S(2)}) %collective-permute-start) | collective-permute-done | bytes 245792 | tf_op jit(solution)/shard_map/ppermute | solution.py:357
  40.8 0.1 slice_sum.1
  40.9 0.4 collective-permute-start.1
  41.3 1.7 %collective-permute-start.2 = (bf16[40,768]{1,0:T(8,128)(2,1)S(1)}, bf16[40,768]{1,0:T(8,128)(2,1)S(1)}, u32[]{:S(2)}, u32[]{:S(2)}) collective-permute-start(bf16[40,768]{1,0:T(8,128)(2,1)S(1)} %get-tuple-element.14), channel_id=1, source_target_pairs={{0,16},{8,24},{16,0},{24,8},{1,17},{9,25},{17,1},{25,9},{2,18},{10... | collective-permute-start | bytes 184328 | tf_op jit(solution)/shard_map/ppermute | solution.py:357
  43.0 1.5 %collective-permute-start.3 = (bf16[40,768]{1,0:T(8,128)(2,1)S(1)}, bf16[40,768]{1,0:T(8,128)(2,1)S(1)}, u32[]{:S(2)}, u32[]{:S(2)}) collective-permute-start(bf16[40,768]{1,0:T(8,128)(2,1)S(1)} %get-tuple-element.15), channel_id=1, source_target_pairs={{0,24},{8,16},{16,8},{24,0},{1,25},{9,17},{17,9},{25,1},{2,26},{10... | collective-permute-start | bytes 184328 | tf_op jit(solution)/shard_map/ppermute | solution.py:357
  44.5 14.1 %other_tangent.1 = (bf16[8,40,768]{2,1,0:T(8,128)(2,1)S(1)}, f32[8,128]{1,0:T(8,128)S(1)}) custom-call(bf16[40,1024]{1,0:T(8,128)(2,1)S(1)} %hidden.1.h_ref, bf16[2,1024,6144]{2,1,0:T(8,128)(2,1)} %v_ref.5), custom_call_target="tpu_custom_call" | custom-call | flops 503316480 | bytes 25165824 | tf_op jit(solution)/shard_map/other_tangent/pallas_call | solution.py:168
  58.6 0.0 collective-permute-done.1.refs_1_
  58.6 0.0 collective-permute-done.2.refs_2_
  58.6 0.0 collective-permute-done.3.refs_3_
  58.7 3.7 %collective-permute-start.6 = (bf16[40,768]{1,0:T(8,128)(2,1)S(1)}, bf16[40,768]{1,0:T(8,128)(2,1)S(1)}, u32[]{:S(2)}, u32[]{:S(2)}) collective-permute-start(bf16[40,768]{1,0:T(8,128)(2,1)S(1)} %get-tuple-element.17.refs_0_), channel_id=1, source_target_pairs={{0,6},{2,4},{4,2},{6,0},{1,7},{3,5},{5,3},{7,1},{8,14},{10,12},{12... | collective-permute-start | bytes 184328 | tf_op jit(solution)/shard_map/ppermute | solution.py:357
  62.3 0.0 collective-permute-start.5
  62.4 0.8 collective-permute-start.4
  63.1 0.1 select_reduce_fusion.1
  63.2 0.1 mul.40.rho_ref
  63.3 2.0 %collective-permute-done.6.refs_3_ = bf16[40,768]{1,0:T(8,128)(2,1)S(1)} collective-permute-done((bf16[40,768]{1,0:T(8,128)(2,1)S(1)}, bf16[40,768]{1,0:T(8,128)(2,1)S(1)}, u32[]{:S(2)}, u32[]{:S(2)}) %collective-permute-start.6) | collective-permute-done | bytes 61472 | tf_op jit(solution)/shard_map/ppermute | solution.py:357
  65.3 2.2 %collective-permute-done.5.refs_2_ = bf16[40,768]{1,0:T(8,128)(2,1)S(1)} collective-permute-done((bf16[40,768]{1,0:T(8,128)(2,1)S(1)}, bf16[40,768]{1,0:T(8,128)(2,1)S(1)}, u32[]{:S(2)}, u32[]{:S(2)}) %collective-permute-start.5) | collective-permute-done | bytes 61472 | tf_op jit(solution)/shard_map/ppermute | solution.py:357
  67.5 0.0 collective-permute-done.4.refs_1_
  67.5 0.4 cotangent.1
  67.9 8.7 %all-gather = bf16[320,768]{1,0:T(8,128)(2,1)S(1)} all-gather(bf16[40,768]{1,0:T(8,128)(2,1)S(1)} %cotangent.1), channel_id=2, replica_groups=mesh['dp'=4,'group'=4,'slice'=2] {'dp','slice'}, dimensions={0}, use_global_device_ids=true | all-gather | bytes 552960 | tf_op jit(solution)/shard_map/all_gather | solution.py:403
  76.6 1.0 products.1
  77.7 0.7 broadcast_in_dim.82
  78.3 3.8 %all-to-all-start = ((f32[32,8,128]{2,1,0:T(8,128)}), f32[32,8,128]{2,1,0:T(8,128)S(1)}, u32[]{:S(2)}, u32[]{:S(2)}) async-start(f32[32,8,128]{2,1,0:T(8,128)} %broadcast_in_dim.82), calls=%async_computation | async-start | bytes 262144 | tf_op jit(solution)/shard_map/all_to_all | solution.py:407
  82.2 0.2 copy.18
  82.3 8.0 %all-to-all-done.parts_ref = f32[32,8,128]{2,1,0:T(8,128)S(1)} async-done(((f32[32,8,128]{2,1,0:T(8,128)}), f32[32,8,128]{2,1,0:T(8,128)S(1)}, u32[]{:S(2)}, u32[]{:S(2)}) %all-to-all-start) | async-done | bytes 131104 | tf_op jit(solution)/shard_map/all_to_all | solution.py:407
  90.3 16.6 %residual.1 = (bf16[1024,6144]{1,0:T(8,128)(2,1)}, f32[8,128]{1,0:T(8,128)S(1)}) custom-call(f32[32,8,128]{2,1,0:T(8,128)S(1)} %all-to-all-done.parts_ref, bf16[1024,40]{1,0:T(8,128)(2,1)S(1)} %bitcast.10, bf16[8,40,768]{2,1,0:T(8,128)(2,1)S(1)} %bitcast.9, bf16[2,1024,6144]{2,1,0:T(8,128)(2,1)} %v_ref.5), custom_call_target="tpu_custom_call" | custom-call | flops 503316480 | bytes 37748736 | tf_op jit(solution)/shard_map/residual/pallas_call | solution.py:329
  107.0 0.6 copy.19
  (17 shorter events, 0.2 us)
Async XLA Ops:
  30.6 8.8 %copy-start = (f32[6144]{0:T(1024)S(1)}, f32[6144]{0:T(1024)}, u32[]{:S(2)}) copy-start(f32[6144]{0:T(1024)} %param.15) | copy-start | bytes 73732
  30.6 8.8 %copy-start.1 = (f32[16]{0:T(128)S(1)}, f32[16]{0:T(128)}, u32[]{:S(2)}) copy-start(f32[16]{0:T(128)} %param.14) | copy-start | bytes 196
  39.3 1.6 %collective-permute-start = (bf16[4,40,768]{2,1,0:T(8,128)(2,1)S(1)}, bf16[4,40,768]{2,1,0:T(8,128)(2,1)S(1)}, u32[]{:S(2)}, u32[]{:S(2)}) collective-permute-start(bf16[4,40,768]{2,1,0:T(8,128)(2,1)S(1)} %get-tuple-element.26), channel_id=1, source_target_pairs={{0,1},{1,0},{2,3},{3,2},{4,5},{5,4},{6,7},{7,6},{8,9},{9,8},{10,11... | collective-permute-start | bytes 737288 | tf_op jit(solution)/shard_map/ppermute | solution.py:357
  40.9 17.7 %collective-permute-start.1 = (bf16[40,768]{1,0:T(8,128)(2,1)S(1)}, bf16[40,768]{1,0:T(8,128)(2,1)S(1)}, u32[]{:S(2)}, u32[]{:S(2)}) collective-permute-start(bf16[40,768]{1,0:T(8,128)(2,1)S(1)} %get-tuple-element.13), channel_id=1, source_target_pairs={{0,8},{8,0},{16,24},{24,16},{1,9},{9,1},{17,25},{25,17},{2,10},{10... | collective-permute-start | bytes 184328 | tf_op jit(solution)/shard_map/ppermute | solution.py:357
  41.3 17.3 %collective-permute-start.2 = (bf16[40,768]{1,0:T(8,128)(2,1)S(1)}, bf16[40,768]{1,0:T(8,128)(2,1)S(1)}, u32[]{:S(2)}, u32[]{:S(2)}) collective-permute-start(bf16[40,768]{1,0:T(8,128)(2,1)S(1)} %get-tuple-element.14), channel_id=1, source_target_pairs={{0,16},{8,24},{16,0},{24,8},{1,17},{9,25},{17,1},{25,9},{2,18},{10... | collective-permute-start | bytes 184328 | tf_op jit(solution)/shard_map/ppermute | solution.py:357
  43.0 15.6 %collective-permute-start.3 = (bf16[40,768]{1,0:T(8,128)(2,1)S(1)}, bf16[40,768]{1,0:T(8,128)(2,1)S(1)}, u32[]{:S(2)}, u32[]{:S(2)}) collective-permute-start(bf16[40,768]{1,0:T(8,128)(2,1)S(1)} %get-tuple-element.15), channel_id=1, source_target_pairs={{0,24},{8,16},{16,8},{24,0},{1,25},{9,17},{17,9},{25,1},{2,26},{10... | collective-permute-start | bytes 184328 | tf_op jit(solution)/shard_map/ppermute | solution.py:357
  58.7 6.6 %collective-permute-start.6 = (bf16[40,768]{1,0:T(8,128)(2,1)S(1)}, bf16[40,768]{1,0:T(8,128)(2,1)S(1)}, u32[]{:S(2)}, u32[]{:S(2)}) collective-permute-start(bf16[40,768]{1,0:T(8,128)(2,1)S(1)} %get-tuple-element.17.refs_0_), channel_id=1, source_target_pairs={{0,6},{2,4},{4,2},{6,0},{1,7},{3,5},{5,3},{7,1},{8,14},{10,12},{12... | collective-permute-start | bytes 184328 | tf_op jit(solution)/shard_map/ppermute | solution.py:357
  62.3 5.1 %collective-permute-start.5 = (bf16[40,768]{1,0:T(8,128)(2,1)S(1)}, bf16[40,768]{1,0:T(8,128)(2,1)S(1)}, u32[]{:S(2)}, u32[]{:S(2)}) collective-permute-start(bf16[40,768]{1,0:T(8,128)(2,1)S(1)} %get-tuple-element.17.refs_0_), channel_id=1, source_target_pairs={{0,4},{2,6},{4,0},{6,2},{1,5},{3,7},{5,1},{7,3},{8,12},{10,14},{12... | collective-permute-start | bytes 184328 | tf_op jit(solution)/shard_map/ppermute | solution.py:357
  62.4 5.1 %collective-permute-start.4 = (bf16[40,768]{1,0:T(8,128)(2,1)S(1)}, bf16[40,768]{1,0:T(8,128)(2,1)S(1)}, u32[]{:S(2)}, u32[]{:S(2)}) collective-permute-start(bf16[40,768]{1,0:T(8,128)(2,1)S(1)} %get-tuple-element.17.refs_0_), channel_id=1, source_target_pairs={{0,2},{2,0},{4,6},{6,4},{1,3},{3,1},{5,7},{7,5},{8,10},{10,8},{12,... | collective-permute-start | bytes 184328 | tf_op jit(solution)/shard_map/ppermute | solution.py:357
  78.3 12.0 %all-to-all-start = ((f32[32,8,128]{2,1,0:T(8,128)}), f32[32,8,128]{2,1,0:T(8,128)S(1)}, u32[]{:S(2)}, u32[]{:S(2)}) async-start(f32[32,8,128]{2,1,0:T(8,128)} %broadcast_in_dim.82), calls=%async_computation | async-start | bytes 262144 | tf_op jit(solution)/shard_map/all_to_all | solution.py:407

commit v2 on v1

v2 whole, which is shorter than its diff:
```python
import functools
import math

import jax
import jax.numpy as jnp
from jax import lax
from jax.experimental import pallas as pl
from jax.experimental.pallas import tpu as pltpu
from jax.sharding import Mesh, PartitionSpec as P

FF = 8192
E = 4
BASIS = 2
STEPS = 1
CAP = 9
MIB = 1 << 20
F32 = jnp.float32
BF16 = jnp.bfloat16
PLANE = ("dp", "slice")
EVERY = ("dp", "group", "slice")


def params(mib=None):
    return pltpu.CompilerParams(vmem_limit_bytes=mib * MIB if mib else None)


def pinned(*arrays):
    return tuple(pltpu.with_memory_space_constraint(x, pltpu.VMEM) for x in arrays)


def dot(a, b, dims=((1,), (0,))):
    return lax.dot_general(a, b, (dims, ((), ())), preferred_element_type=F32)


def divisor(total, unit, limit):
    best = unit
    for size in range(unit, limit + 1, unit):
        if total % size == 0:
            best = size
    return best


def load_kernel(tok_dev, ids_ref, routes_ref, gates_ref, rho_ref, sigma_ref, wg_hbm, wu_hbm, *outs):
    wg_ref, wu_ref, place_ref, gate_ref, rho_row_ref, sigma_row_ref, sems = outs
    source, group, chunk = ids_ref[0], ids_ref[1], ids_ref[2]
    blocks = sems.shape[1]
    depth = wg_ref.shape[0] // blocks
    copies = []
    for i in range(blocks):
        at = pl.ds(i * depth, depth)
        copies.append(pltpu.make_async_copy(wg_hbm.at[at], wg_ref.at[at], sems.at[0, i]))
        copies.append(pltpu.make_async_copy(wu_hbm.at[at], wu_ref.at[at], sems.at[1, i]))
    for copy in copies:
        copy.start()

    experts, rows, total = place_ref.shape
    routes, gates = routes_ref[...], gates_ref[...]
    first = lax.broadcasted_iota(jnp.int32, (total, total), 0)
    second = lax.broadcasted_iota(jnp.int32, (total, total), 1)
    earlier = ((first // tok_dev == second // tok_dev) & (first < second)).astype(F32).astype(BF16)
    expert = lax.broadcasted_iota(jnp.int32, (8, total), 0) ^ group
    member = jnp.zeros((8, total), F32)
    for k in range(routes.shape[0]):
        member = member + (routes[k : k + 1, :] == expert).astype(F32)
    rank = dot(member.astype(BF16), earlier).astype(jnp.int32)
    start = (lax.broadcasted_iota(jnp.int32, (8, total), 1) // tok_dev) * CAP
    slot = jnp.where(member > 0.0, start + rank, -1)
    row = lax.broadcasted_iota(jnp.int32, (rows, total), 0)
    places = [(slot[e : e + 1, :] == row).astype(F32).astype(BF16) for e in range(experts)]
    swapped = (first // tok_dev == (second // tok_dev) ^ source) & (first % tok_dev == second % tok_dev)
    for e in range(experts):
        place_ref[e] = dot(places[e], swapped.astype(F32).astype(BF16)).astype(BF16)
    gate = jnp.zeros((1, total), F32)
    for k in range(routes.shape[0]):
        gate = gate + jnp.where(routes[k : k + 1, :] == group, gates[k : k + 1, :], 0.0)
    gate_ref[...] = jnp.sum(jnp.where(swapped, gate, 0.0), axis=1, keepdims=True)
    wide = rho_row_ref.shape[1]
    rho_row_ref[...] = jnp.zeros_like(rho_row_ref)
    rho_row_ref[:, 0:tok_dev] = rho_ref[...]
    sigma_row_ref[...] = sigma_ref[:, pl.ds(pl.multiple_of(chunk * wide, 128), wide)]

    for copy in copies:
        copy.wait()


def load_call(ids, routes, gates, rho, sigma, w_gate, w_up, tok_dev, rows, wide):
    features, units = w_gate.shape
    total = routes.shape[1]
    blocks = features // divisor(features, 128, 1024)
    vmem = pl.BlockSpec(memory_space=pltpu.VMEM)
    hbm = pl.BlockSpec(memory_space=pltpu.HBM)
    return pl.pallas_call(
        functools.partial(load_kernel, tok_dev),
        in_specs=[pl.BlockSpec(memory_space=pltpu.SMEM), vmem, vmem, vmem, vmem, hbm, hbm],
        out_specs=[vmem] * 6,
        out_shape=[
            pltpu.VMEM((features, units), BF16),
            pltpu.VMEM((features, units), BF16),
            jax.ShapeDtypeStruct((E, rows, total), BF16),
            jax.ShapeDtypeStruct((total, 1), F32),
            jax.ShapeDtypeStruct((1, wide), F32),
            jax.ShapeDtypeStruct((1, wide), F32),
        ],
        scratch_shapes=[pltpu.SemaphoreType.DMA((2, blocks))],
        compiler_params=params(3),
        cost_estimate=pl.CostEstimate(flops=0, bytes_accessed=8 * features * units, transcendentals=0),
        name="load",
    )(ids, routes, gates, rho, sigma, w_gate, w_up)


def hidden_kernel(scale, parts, cuts, column_ref, *refs):
    xs, (wg_ref, wu_ref, gate_ref, place_ref, v_hbm) = refs[:parts], refs[parts : parts + 5]
    outs = refs[parts + 5 :]
    h_ref, v_ref, tangents = outs[0], outs[1], outs[2 : 2 + cuts]
    acc_g, acc_u, sems = outs[2 + cuts :]
    units, features = v_ref.shape
    blocks = sems.shape[0]
    copies = []
    for i in range(blocks):
        at = pl.ds(i * (units // blocks), units // blocks)
        copies.append(pltpu.make_async_copy(v_hbm.at[BASIS - 1, at], v_ref.at[at], sems.at[i]))
    for copy in copies:
        copy.start()

    depth = divisor(features, 128, 1024)
    for i in range(features // depth):
        at = pl.ds(i * depth, depth)
        x = jnp.concatenate([ref[:, at] for ref in xs], axis=0)
        part_g, part_u = dot(x, wg_ref[at, :]), dot(x, wu_ref[at, :])
        if i:
            acc_g[...] += part_g
            acc_u[...] += part_u
        else:
            acc_g[...] = part_g
            acc_u[...] = part_u
    g = acc_g[...]
    full = (g * (1.0 / (1.0 + jnp.exp(-g))) * acc_u[...] * gate_ref[...]).astype(BF16)
    h = dot(place_ref[0], full).astype(BF16)
    h_ref[...] = h

    for copy in copies:
        copy.wait()
    wide = tangents[0].shape[2]
    for j, out_ref in enumerate(tangents):
        for d in range(out_ref.shape[0]):
            start = pl.multiple_of(column_ref[j * out_ref.shape[0] + d] * wide, 128)
            out_ref[d] = (dot(h, v_ref[:, pl.ds(start, wide)]) * scale).astype(out_ref.dtype)


def hidden_call(column, xs, wg, wu, gate, place, basis, cuts, scale):
    _, units, features = basis.shape
    _, rows, total = place.shape
    sources = len(xs)
    wide = features // (cuts * sources)
    blocks = 4 if units % 64 == 0 else 1
    vmem = pl.BlockSpec(memory_space=pltpu.VMEM)
    hbm = pl.BlockSpec(memory_space=pltpu.HBM)
    wg, wu = pinned(wg, wu)
    return pl.pallas_call(
        functools.partial(hidden_kernel, scale, sources, cuts),
        in_specs=[pl.BlockSpec(memory_space=pltpu.SMEM)] + [vmem] * (sources + 4) + [hbm],
        out_specs=[vmem] * (2 + cuts),
        out_shape=[
            jax.ShapeDtypeStruct((rows, units), BF16),
            pltpu.VMEM((units, features), BF16),
        ]
        + [jax.ShapeDtypeStruct((sources, rows, wide), BF16 if j else F32) for j in range(cuts)],
        scratch_shapes=[pltpu.VMEM((total, units), F32)] * 2 + [pltpu.SemaphoreType.DMA((blocks,))],
        compiler_params=params(8),
        cost_estimate=pl.CostEstimate(
            flops=6 * rows * features * units, bytes_accessed=6 * features * units, transcendentals=0
        ),
        name="hidden",
    )(column, *xs, wg, wu, gate, place, basis)


def products_of(pairs, reads, units, features):
    strip = 32 if units % 32 == 0 else units
    wide = 256

    def fold(x):
        return jnp.sum(x.reshape(strip // 8, 8, wide), axis=0)

    def column(q, carry):
        across = pl.ds(pl.multiple_of(q * wide, 128), wide)

        def body(i, sums):
            at = pl.ds(pl.multiple_of(i * strip, strip), strip)
            values = [ref[at, across].astype(F32) for ref in reads]
            return tuple(s + fold(values[a] * values[b]) for s, (a, b) in zip(sums, pairs))

        return lax.fori_loop(0, units // strip, body, carry, unroll=4 if units // strip % 4 == 0 else 1)

    zero = jnp.zeros((8, wide), F32)
    return lax.fori_loop(0, features // wide, column, (zero,) * len(pairs))


def other_kernel(scale, h_ref, v_hbm, after_ref, held_ref, v_ref, t_ref, ht_ref, gram_ref, acc, sems):
    units, features = v_ref.shape
    blocks = sems.shape[0]
    depth = units // blocks
    copies = []
    for i in range(blocks):
        at = pl.ds(i * depth, depth)
        copies.append(pltpu.make_async_copy(v_hbm.at[0, at], v_ref.at[at], sems.at[i]))
    for copy in copies:
        copy.start()
    ht_ref[...] = h_ref[...].astype(F32).T.astype(BF16)
    chunks, _, wide = t_ref.shape
    sums = None
    for i in range(blocks):
        at = pl.ds(i * depth, depth)
        copies[i].wait()
        for c in range(chunks):
            across = pl.ds(c * wide, wide)
            part = dot(h_ref[:, at], v_ref[at, across])
            if i:
                part = part + acc[:, across]
            if i < blocks - 1:
                acc[:, across] = part
            else:
                t_ref[c] = (part * scale).astype(BF16)
        (square,) = products_of(((0, 0),), (v_ref.at[at],), depth, features)
        sums = square if sums is None else sums + square
    gram_ref[...] = sums


def other_call(hidden, basis, after, held, chunks, scale):
    rows, units = hidden.shape
    features = basis.shape[2]
    blocks = 4 if units % 512 == 0 else 1
    vmem = pl.BlockSpec(memory_space=pltpu.VMEM)
    hbm = pl.BlockSpec(memory_space=pltpu.HBM)
    return pl.pallas_call(
        functools.partial(other_kernel, scale),
        in_specs=[vmem, hbm, hbm, vmem],
        out_specs=[vmem] * 4,
        out_shape=[
            pltpu.VMEM((units, features), BF16),
            jax.ShapeDtypeStruct((chunks, rows, features // chunks), BF16),
            jax.ShapeDtypeStruct((units, rows), BF16),
            jax.ShapeDtypeStruct((8, 256), F32),
        ],
        scratch_shapes=[pltpu.VMEM((rows, features), F32), pltpu.SemaphoreType.DMA((blocks,))],
        compiler_params=params(5),
        cost_estimate=pl.CostEstimate(
            flops=2 * rows * features * units, bytes_accessed=2 * features * units, transcendentals=0
        ),
        name="other_tangent",
    )(hidden, basis, after, *pinned(held))


def gram_kernel(v0_ref, v1_ref, after_ref, out_ref):
    units, features = v0_ref.shape
    out_ref[0], out_ref[1] = products_of(((0, 1), (1, 1)), (v0_ref, v1_ref), units, features)


def gram_call(v0, v1, after):
    vmem = pl.BlockSpec(memory_space=pltpu.VMEM)
    v0, v1 = pinned(v0, v1)
    return pl.pallas_call(
        gram_kernel,
        in_specs=[vmem, vmem, pl.BlockSpec(memory_space=pltpu.HBM)],
        out_specs=vmem,
        out_shape=jax.ShapeDtypeStruct((2, 8, 256), F32),
        compiler_params=params(2),
        cost_estimate=pl.CostEstimate(
            flops=4 * v0.shape[0] * v0.shape[1], bytes_accessed=4 * v0.shape[0] * v0.shape[1], transcendentals=0
        ),
        name="gram",
    )(v0, v1, after)


def pieces(x):
    first = x.astype(BF16)
    rest = x - first.astype(F32)
    second = rest.astype(BF16)
    return first, second, (rest - second.astype(F32)).astype(BF16)


def share_kernel(line, parts, *refs):
    ins, rho_ref, outs = refs[:parts], refs[parts], refs[parts + 2 :]
    rows, wide = ins[0].shape[1:]
    row = lax.broadcasted_iota(jnp.int32, (rows, wide), 0)
    for j, out_ref in enumerate(outs):
        total = ins[0][j].astype(F32)
        for ref in ins[1:]:
            total = total + ref[j].astype(F32)
        if j:
            for n, piece in enumerate(pieces(rho_ref[...])):
                total = jnp.where(row == line + n, piece.astype(F32), total)
        out_ref[...] = total.astype(out_ref.dtype)


def share_call(parts, rho_row, line, held):
    sources, rows, wide = parts[0].shape
    return pl.pallas_call(
        functools.partial(share_kernel, line, len(parts)),
        in_specs=[pl.BlockSpec(memory_space=pltpu.VMEM)] * (len(parts) + 2),
        out_shape=[jax.ShapeDtypeStruct((rows, wide), BF16 if j else F32) for j in range(sources)],
        compiler_params=params(6),
        name="slice_sum",
    )(*parts, rho_row, *pinned(held))


def sum_kernel(line, *refs):
    ins, rho_own, out_ref, rho_ref = refs[:-5], refs[-5], refs[-2], refs[-1]
    total = ins[0][...]
    rho_ref[0:1, :] = rho_own[:, 0:128]
    for j, ref in enumerate(ins[1:]):
        part = ref[...].astype(F32)
        total = total + part
        rho_ref[j + 1 : j + 2, :] = (
            part[line : line + 1, 0:128] + part[line + 1 : line + 2, 0:128] + part[line + 2 : line + 3, 0:128]
        )
    row = lax.broadcasted_iota(jnp.int32, total.shape, 0)
    out_ref[...] = jnp.where(row < line, total, 0.0).astype(BF16)


def sum_call(parts, rho_row, line, held):
    rows, wide = parts[0].shape
    return pl.pallas_call(
        functools.partial(sum_kernel, line),
        in_specs=[pl.BlockSpec(memory_space=pltpu.VMEM)] * (len(parts) + 3),
        out_shape=[
            jax.ShapeDtypeStruct((rows, wide), BF16),
            jax.ShapeDtypeStruct((len(parts), 128), F32),
        ],
        compiler_params=params(6),
        name="plane_sum",
    )(*parts, rho_row, *pinned(*held))


def cotangent_kernel(parts, kappa, place_ref, rho_ref, sigma_ref, *refs):
    ins, out_ref = refs[:parts], refs[-1]
    response = None
    for j, ref in enumerate(ins):
        term = dot(place_ref[j], ref[...], ((0,), (0,)))
        response = term if response is None else response + term
    sources, tok_dev = rho_ref.shape[0], response.shape[0] // rho_ref.shape[0]
    down = lax.broadcasted_iota(jnp.int32, (tok_dev, 128), 0)
    across = lax.broadcasted_iota(jnp.int32, (tok_dev, 128), 1)
    columns = [
        jnp.sum(jnp.where(down == across, rho_ref[j : j + 1, :], 0.0), axis=1, keepdims=True)
        for j in range(sources)
    ]
    rho = jnp.concatenate(columns, axis=0)
    cot = (kappa * rho * sigma_ref[...] * response).astype(BF16)
    out_ref[...] = dot(place_ref[0], cot).astype(BF16)


def cotangent_call(parts, placing, rho_all, sigma_row, kappa, held):
    return pl.pallas_call(
        functools.partial(cotangent_kernel, len(parts), kappa),
        in_specs=[pl.BlockSpec(memory_space=pltpu.VMEM)] * (len(parts) + 5),
        out_shape=jax.ShapeDtypeStruct(parts[0].shape, BF16),
        compiler_params=params(6),
        name="cotangent",
    )(placing, rho_all, sigma_row, *parts, *pinned(*held))


def products_kernel(scale, column_ref, h_ref, c_ref, t0_ref, square_ref, gram_ref, *refs):
    tangents, out_ref = refs[:-1], refs[-1]
    rows = c_ref.shape[1]
    h = h_ref[...]
    weight = dot(h, h, ((1,), (1,)))
    c0 = jnp.zeros(c_ref.shape[1:], F32)
    c1 = jnp.zeros(c_ref.shape[1:], F32)
    square = jnp.zeros((rows, rows), F32)
    place = 0
    for t_ref in tangents:
        for d in range(t_ref.shape[0]):
            c = column_ref[place]
            place += 1
            cot = c_ref[c]
            wide = cot.astype(F32)
            c0 = c0 + wide * t0_ref[c].astype(F32)
            c1 = c1 + wide * t_ref[d].astype(F32)
            square = square + dot(cot, cot, ((1,), (1,)))
    values = (
        jnp.sum(c0),
        jnp.sum(c1),
        jnp.sum(weight * square) * (scale * scale),
        jnp.sum(square_ref[...]),
        jnp.sum(gram_ref[0]),
        jnp.sum(gram_ref[1]),
    )
    lane = lax.broadcasted_iota(jnp.int32, out_ref.shape, 2)
    out = jnp.zeros(out_ref.shape, F32)
    for n, value in enumerate(values):
        out = jnp.where(lane == n, value, out)
    out_ref[...] = out


def products_call(column, hidden, cot, t0, square, gram, tangents, scale, devices, held):
    vmem = pl.BlockSpec(memory_space=pltpu.VMEM)
    return pl.pallas_call(
        functools.partial(products_kernel, scale),
        in_specs=[pl.BlockSpec(memory_space=pltpu.SMEM)] + [vmem] * (5 + len(tangents) + len(held)),
        out_specs=vmem,
        out_shape=jax.ShapeDtypeStruct((devices, 1, 128), F32),
        compiler_params=params(8),
        name="products",
    )(column, hidden, cot, t0, square, gram, *tangents, *pinned(*held))


def final_kernel(scale, entries, parts_ref, ht_ref, c_ref, v0_ref, v1_ref, out_ref, hess_ref, scalars):
    units, wide = out_ref.shape

    @pl.when(pl.program_id(0) == 0)
    def _():
        total = jnp.sum(parts_ref[...], axis=0) * (1.0 / entries)
        c0, c1, square = total[:, 0:1], total[:, 1:2], total[:, 2:3]
        g00, g01, g11 = total[:, 3:4], total[:, 4:5], total[:, 5:6]
        norm = square - 2.0 * (c0 * c0 + c1 * c1) + c0 * c0 * g00 + 2.0 * c0 * c1 * g01 + c1 * c1 * g11
        beta = jnp.sqrt(jnp.maximum(norm, square * 2.0**-24))
        line = lax.broadcasted_iota(jnp.int32, (8, 128), 0)
        hess_ref[...] = jnp.where(line == 0, c0, jnp.where(line == 1, c1, beta))
        inverse = 1.0 / beta
        scalars[0] = (c0 * inverse)[0, 0]
        scalars[1] = (c1 * inverse)[0, 0]
        scalars[2] = (scale * inverse)[0, 0]

    a0, a1, s = scalars[0], scalars[1], scalars[2]
    strip = 256 if units % 256 == 0 else units
    across = divisor(wide, 128, 256)
    begin = pl.program_id(0) * wide
    for q in range(wide // across):
        source = pl.ds(pl.multiple_of(begin + q * across, 128), across)
        target = pl.ds(q * across, across)
        cot = c_ref[0, :, target]
        for i in range(units // strip):
            at = pl.ds(i * strip, strip)
            image = dot(ht_ref[at, :], cot)
            out = image * s - a0 * v0_ref[at, source].astype(F32) - a1 * v1_ref[at, source].astype(F32)
            out_ref[at, target] = out.astype(BF16)


def final_call(parts, hidden_t, cot, v0, v1, scale, entries):
    units, rows = hidden_t.shape
    chunks, _, wide = cot.shape
    vmem = pl.BlockSpec(memory_space=pltpu.VMEM)
    v0, v1 = pinned(v0, v1)
    return pl.pallas_call(
        functools.partial(final_kernel, scale, entries),
        grid=(chunks,),
        in_specs=[
            pl.BlockSpec(parts.shape, lambda c: (0, 0, 0)),
            pl.BlockSpec((units, rows), lambda c: (0, 0)),
            pl.BlockSpec((1, rows, wide), lambda c: (c, 0, 0)),
            vmem,
            vmem,
        ],
        out_specs=[
            pl.BlockSpec((units, wide), lambda c: (0, c)),
            pl.BlockSpec((8, 128), lambda c: (0, 0)),
        ],
        out_shape=[
            jax.ShapeDtypeStruct((units, chunks * wide), BF16),
            jax.ShapeDtypeStruct((8, 128), F32),
        ],
        scratch_shapes=[pltpu.SMEM((4,), F32)],
        compiler_params=params(8),
        cost_estimate=pl.CostEstimate(
            flops=2 * rows * units * chunks * wide, bytes_accessed=6 * units * chunks * wide, transcendentals=0
        ),
        name="residual",
    )(parts, hidden_t, cot, v0, v1)


def swap(x, axis, distance):
    size = lax.axis_size(axis)
    return lax.ppermute(x, axis, [(i, i ^ distance) for i in range(size)])


def body(tokens, w_gate, w_up, basis, routes, gates, rho, sigma):
    sources, slices = lax.axis_size("dp"), lax.axis_size("slice")
    source, group, part = lax.axis_index("dp"), lax.axis_index("group"), lax.axis_index("slice")
    tok_dev, features = tokens.shape
    total = tok_dev * sources
    scale = 1.0 / math.sqrt(FF)
    kappa = E * FF / total
    entries = float(E * FF * features)
    line = sources * CAP
    rows = -(-(line + 3) // 8) * 8
    split = features % (slices * sources * 128) == 0
    cuts = slices if split else 1
    chunks = sources * cuts
    wide = features // chunks
    place = jnp.arange(chunks, dtype=jnp.int32)
    lane = part if split else 0
    column = ((place % sources) ^ source) * cuts + ((place // sources) ^ lane)
    ids = jnp.stack([source, group, column[0]]).astype(jnp.int32)
    w_gate, w_up, basis = (pltpu.with_memory_space_constraint(x, pltpu.HBM) for x in (w_gate, w_up, basis))

    xs = [tokens] + [swap(tokens, "dp", j) for j in range(1, sources)]
    wg, wu, placing, gate, rho_row, sigma_row = load_call(
        ids, routes.T, gates.T, rho[None, :], sigma[None, :], w_gate, w_up, tok_dev, rows, wide
    )
    hidden, v1, *tangents = hidden_call(column, xs, wg, wu, gate, placing, basis, cuts, scale)
    if split:
        got = [tangents[0]] + [swap(tangents[j], "slice", j) for j in range(1, slices)]
    else:
        got = [lax.psum(tangents[0], "slice")]
    shares = share_call(got, rho_row, line, v1)
    got = [shares[0]] + [swap(shares[j], "dp", j) for j in range(1, sources)]
    v0, t0, hidden_t, square = other_call(hidden, basis, shares[0], v1, chunks, scale)
    summed, rho_all = sum_call(got, rho_row, line, (v0, v1))
    got = [summed] + [swap(summed, "group", j) for j in range(1, E)]
    gram = gram_call(v0, v1, rho_all)
    cot = cotangent_call(got, placing, rho_all, sigma_row, kappa, (v0, v1))
    cot = lax.all_gather(cot, PLANE if split else "dp", axis=0)

    devices = sources * E * slices
    parts = products_call(column, hidden, cot, t0, square, gram, tangents, scale, devices, ())
    parts = lax.all_to_all(parts, EVERY, 0, 0, tiled=True)
    new, hess = final_call(parts, hidden_t, cot, v0, v1, scale, entries)
    return new, hess[: BASIS + 1, :1]


def solution(mesh):
    sources, experts = mesh.shape["dp"], mesh.shape["expert"]
    fine = Mesh(mesh.devices.reshape(sources, E, experts // E), EVERY)
    units = ("group", "slice", "dp")
    return jax.shard_map(
        body,
        mesh=fine,
        in_specs=(
            P("dp", None),
            P(None, units),
            P(None, units),
            P(None, units, None),
            P(),
            P(),
            P("dp"),
            P(),
        ),
        out_specs=(P(units, None), P()),
        check_vma=False,
    )
```

time: 108 us -> 83.6 us (0.77)
  Pallas kernels: 55.1 us -> 42.7 us
  waiting for transfers between devices: 13.5 us -> 1.52 us
  other arithmetic: 1.99 us -> 0.12 us
  local copies, waits for them, and re-layouts: 1.69 us -> 3.35 us
    all_gather x1 -> x0, blocking collectives: 13.8 us -> none  [body(): everyone = lax.all_gather(tokens, 'dp', axis=0, tiled=True)]
    all_to_all x0 -> x1, blocking collectives: none -> 11.8 us  [body(): parts = lax.all_to_all(parts, EVERY, 0, 0, tiled=True)]
    all_to_all x1 -> x0, waiting for transfers between devices: 8 us -> none  [body(): lax.all_to_all(jnp.broadcast_to(sums, (devices, 8, 128)), EVERY, 0, 0, ti...]
    pallas_call x1, Pallas kernels: 16.6 us -> 9.48 us  [final_call(): pl.pallas_call(functools.partial(final_kernel, scale, entries), grid=(chu...]
    pallas_call x6 -> x7, Pallas kernels: 37.4 us -> 32.2 us  [the longest x1 9.14 us: hidden_call(): pl.pallas_call(functools.partial(hidden_kernel, scale, sources, cuts), in...]
    ppermute x7 -> x10, starting transfers between devices: 8.08 us -> 12.9 us  [swap(): return lax.ppermute(x, axis, [(i, i ^ distance) for i in range(size)])]
    ppermute x7 -> x10, waiting for transfers between devices: 5.54 us -> 1.52 us  [swap(): return lax.ppermute(x, axis, [(i, i ^ distance) for i in range(size)])]
    all_to_all x1 -> x0, starting transfers between devices: 3.84 us -> none  [body(): lax.all_to_all(jnp.broadcast_to(sums, (devices, 8, 128)), EVERY, 0, 0, ti...]
  transfers between devices with their start and end apart: 8 -> 10, of which waited for: 4 -> 1; matrix products, arithmetic and copies ran while one was open for 0% -> 0% of each run, Pallas kernels for 13% -> 27%
where the time goes in v2:
time: 83.6 us; the launch traced here: 83.3 us
  Pallas kernels  42.7 us (51%)
  blocking collectives  21.9 us (26%)
  starting transfers between devices  12.9 us (15%)
  local copies, waits for them, and re-layouts  3.35 us (4%)
  waiting for transfers between devices  1.52 us (2%)
    ppermute x10, starting transfers between devices, swap(): return lax.ppermute(x, axis, [(i, i ^ distance) for i in range(size)])  12.9 us
    all_to_all x1, blocking collectives, body(): parts = lax.all_to_all(parts, EVERY, 0, 0, tiled=True)  11.8 us
    all_gather x1, blocking collectives, body(): cot = lax.all_gather(cot, PLANE if split else 'dp', axis=0)  10 us
    pallas_call x1, Pallas kernels, final_call(): pl.pallas_call(functools.partial(final_kernel, scale, entries), grid=(chu...  9.48 us
    pallas_call x1, Pallas kernels, hidden_call(): pl.pallas_call(functools.partial(hidden_kernel, scale, sources, cuts), in...  9.14 us
    pallas_call x1, Pallas kernels, load_call(): pl.pallas_call(functools.partial(load_kernel, tok_dev), in_specs=[pl.Bloc...  8.93 us
    pallas_call x1, Pallas kernels, other_call(): pl.pallas_call(functools.partial(other_kernel, scale), in_specs=[vmem, hb...  8.16 us
    pallas_call x1, Pallas kernels, gram_call(): pl.pallas_call(gram_kernel, in_specs=[vmem, vmem, pl.BlockSpec(memory_spa...  5.45 us
  transfers between devices with their start and end apart: 10, of which 1 were waited for; matrix products, arithmetic and copies ran while one was open for 0% of the time, Pallas kernels for 27%

profile of v2, /device:TPU:0, one launch (start us, length us, event | category | flops | bytes accessed | tf_op | source)
XLA Modules:
  0.0 83.3 jit_solution(16410209629149172933)
XLA Ops:
  0.6 3.0 %collective-permute-start.1 = (bf16[16,6144]{1,0:T(8,128)(2,1)}, bf16[16,6144]{1,0:T(8,128)(2,1)S(1)}, u32[]{:S(2)}, u32[]{:S(2)}) collective-permute-start(bf16[16,6144]{1,0:T(8,128)(2,1)} %refs_0_.1), channel_id=1, source_target_pairs={{0,16},{8,24},{16,0},{24,8},{1,17},{9,25},{17,1},{25,9},{2,18},{10... | collective-permute-start | bytes 589832 | tf_op jit(solution)/shard_map/ppermute | solution.py:473
  3.7 1.5 %collective-permute-start = (bf16[16,6144]{1,0:T(8,128)(2,1)}, bf16[16,6144]{1,0:T(8,128)(2,1)S(1)}, u32[]{:S(2)}, u32[]{:S(2)}) collective-permute-start(bf16[16,6144]{1,0:T(8,128)(2,1)} %refs_0_.1), channel_id=1, source_target_pairs={{0,8},{8,0},{16,24},{24,16},{1,9},{9,1},{17,25},{25,17},{2,10},{10... | collective-permute-start | bytes 589832 | tf_op jit(solution)/shard_map/ppermute | solution.py:473
  5.2 0.1 collective-permute-start.2
  5.2 0.1 pad_add_fusion.ids_ref
  5.3 0.0 copy-start.1
  5.3 0.7 copy-done.1
  6.1 0.0 copy-start.2
  6.1 0.7 copy-done.2
  6.7 0.0 copy-start.3
  6.7 0.7 copy-done.3
  7.4 0.0 copy-start.4
  7.4 0.7 copy-done.4
  8.1 0.0 copy-start
  8.1 8.9 %load.1 = (bf16[6144,1024]{1,0:T(8,128)(2,1)S(1)}, bf16[6144,1024]{1,0:T(8,128)(2,1)S(1)}, bf16[4,40,64]{2,1,0:T(8,128)(2,1)S(1)}, f32[64,1]{1,0:T(8,128)S(1)}, ...) custom-call(s32[3]{0:T(128)S(1)} %pad_add_fusion.ids_ref, s32[2,64]{1,0:T(2,128)S(1)} %bitcast.12, f32[2,64]{1,0:T(2,128)S(1)} %bitcast.13, ...), custom_call_target="tpu_custom_call" | custom-call | bytes 50331648 | tf_op jit(solution)/shard_map/load/pallas_call | solution.py:92
  17.0 0.0 collective-permute-done.1.refs_2_
  17.0 0.0 collective-permute-done.refs_1_
  17.0 0.0 collective-permute-done.2.refs_3_
  17.0 0.0 copy-done
  17.1 9.1 %hidden.1 = (bf16[40,1024]{1,0:T(8,128)(2,1)S(1)}, bf16[1024,6144]{1,0:T(8,128)(2,1)S(1)}, f32[4,40,768]{2,1,0:T(8,128)S(1)}, bf16[4,40,768]{2,1,0:T(8,128)(2,1)S(1)}) custom-call(s32[8]{0:T(128)S(1)} %fusion.2.column_ref, bf16[16,6144]{1,0:T(8,128)(2,1)S(1)} %copy-done, bf16[16,6144]{1,0:T(8,128)(2,1)S(1)} %collective-permute-done.refs_1_, ...), custom_call_target="tpu_custom_call" | custom-call | flops 1509949440 | bytes 37748736 | tf_op jit(solution)/shard_map/hidden/pallas_call | solution.py:159
  26.2 0.1 collective-permute-start.3
  26.3 1.5 %collective-permute-done.3.refs_1_ = bf16[4,40,768]{2,1,0:T(8,128)(2,1)S(1)} collective-permute-done((bf16[4,40,768]{2,1,0:T(8,128)(2,1)S(1)}, bf16[4,40,768]{2,1,0:T(8,128)(2,1)S(1)}, u32[]{:S(2)}, u32[]{:S(2)}) %collective-permute-start.3) | collective-permute-done | bytes 245792 | tf_op jit(solution)/shard_map/ppermute | solution.py:473
  27.8 0.1 slice_sum.1
  27.8 2.0 %collective-permute-start.4 = (bf16[40,768]{1,0:T(8,128)(2,1)S(1)}, bf16[40,768]{1,0:T(8,128)(2,1)S(1)}, u32[]{:S(2)}, u32[]{:S(2)}) collective-permute-start(bf16[40,768]{1,0:T(8,128)(2,1)S(1)} %get-tuple-element.34), channel_id=1, source_target_pairs={{0,8},{8,0},{16,24},{24,16},{1,9},{9,1},{17,25},{25,17},{2,10},{10... | collective-permute-start | bytes 184328 | tf_op jit(solution)/shard_map/ppermute | solution.py:473
  29.8 1.5 %collective-permute-start.5 = (bf16[40,768]{1,0:T(8,128)(2,1)S(1)}, bf16[40,768]{1,0:T(8,128)(2,1)S(1)}, u32[]{:S(2)}, u32[]{:S(2)}) collective-permute-start(bf16[40,768]{1,0:T(8,128)(2,1)S(1)} %get-tuple-element.35), channel_id=1, source_target_pairs={{0,16},{8,24},{16,0},{24,8},{1,17},{9,25},{17,1},{25,9},{2,18},{10... | collective-permute-start | bytes 184328 | tf_op jit(solution)/shard_map/ppermute | solution.py:473
  31.3 0.1 collective-permute-start.6
  31.4 8.2 %other_tangent.1 = (bf16[1024,6144]{1,0:T(8,128)(2,1)S(1)}, bf16[8,40,768]{2,1,0:T(8,128)(2,1)S(1)}, bf16[1024,40]{1,0:T(8,128)(2,1)S(1)}, f32[8,256]{1,0:T(8,128)S(1)}) custom-call(bf16[40,1024]{1,0:T(8,128)(2,1)S(1)} %get-tuple-element.28.h_ref, bf16[2,1024,6144]{2,1,0:T(8,128)(2,1)} %v_hbm.1, f32[40,768]{1,0:T(8,128)S(1)} %get-tuple-element.33.after_ref.refs_0_, ...), custom_call_target="tpu_custom_call" | custom-call | flops 503316480 | bytes 12582912 | tf_op jit(solution)/shard_map/other_tangent/pallas_call | solution.py:234
  39.6 0.0 collective-permute-done.4.refs_1_
  39.6 0.0 collective-permute-done.5.refs_2_
  39.6 0.0 collective-permute-done.6.refs_3_
  39.6 4.1 %collective-permute-start.9 = (bf16[40,768]{1,0:T(8,128)(2,1)S(1)}, bf16[40,768]{1,0:T(8,128)(2,1)S(1)}, u32[]{:S(2)}, u32[]{:S(2)}) collective-permute-start(bf16[40,768]{1,0:T(8,128)(2,1)S(1)} %get-tuple-element.40.refs_0_), channel_id=1, source_target_pairs={{0,6},{2,4},{4,2},{6,0},{1,7},{3,5},{5,3},{7,1},{8,14},{10,12},{12... | collective-permute-start | bytes 184328 | tf_op jit(solution)/shard_map/ppermute | solution.py:473
  43.7 0.0 collective-permute-start.8
  43.7 0.6 collective-permute-start.7
  44.4 5.5 %gram.1.gram_ref = f32[2,8,256]{2,1,0:T(8,128)S(1)} custom-call(bf16[1024,6144]{1,0:T(8,128)(2,1)S(1)} %get-tuple-element.37.refs_5_.refs_4_.v0_ref, bf16[1024,6144]{1,0:T(8,128)(2,1)S(1)} %get-tuple-element.32.refs_3_.held_ref.refs_6_.refs_5_.v1_ref, f32[4,128]{1,0:T(4,128)S(1)} %get-tuple-element.38.rho_ref.after_ref), custom_call_target="tpu_custom_call" | custom-call | flops 25165824 | bytes 25165824 | tf_op jit(solution)/shard_map/gram/pallas_call | solution.py:261
  49.8 0.0 collective-permute-done.9.refs_3_
  49.9 0.0 collective-permute-done.8.refs_2_
  49.9 0.0 collective-permute-done.7.refs_1_
  49.9 0.4 cotangent.1
  50.3 10.0 %all-gather = bf16[320,768]{1,0:T(8,128)(2,1)S(1)} all-gather(bf16[40,768]{1,0:T(8,128)(2,1)S(1)} %cotangent.1), channel_id=2, replica_groups=mesh['dp'=4,'group'=4,'slice'=2] {'dp','slice'}, dimensions={0}, use_global_device_ids=true | all-gather | bytes 552960 | tf_op jit(solution)/shard_map/all_gather | solution.py:512
  60.3 1.0 %products.1 = f32[32,1,128]{2,1,0:T(1,128)S(1)} custom-call(s32[8]{0:T(128)S(1)} %fusion.2.column_ref, bf16[40,1024]{1,0:T(8,128)(2,1)S(1)} %get-tuple-element.28.h_ref, bf16[8,40,768]{2,1,0:T(8,128)(2,1)S(1)} %bitcast.8, bf16[8,40,768]{2,1,0:T(8,128)(2,1)S(1)} %get-tuple-element.41.t0_ref, f32[8,256]{1,0:T(8,128)S(1)} %get-tuple-element.42.square_ref, ...), custom_call_target="tpu_custom_call" | custom-call | tf_op jit(solution)/shard_map/products/pallas_call | solution.py:397
  61.4 11.8 %all_to_all.5.parts_ref = f32[32,1,128]{2,1,0:T(1,128)S(1)} all-to-all(f32[32,1,128]{2,1,0:T(1,128)S(1)} %products.1), channel_id=1, replica_groups=mesh['dp'=4,'group'=4,'slice'=2] {'dp','group','slice'}, dimensions={0} | all-to-all | bytes 32768 | tf_op jit(solution)/shard_map/all_to_all | solution.py:516
  73.2 9.5 %residual.1 = (bf16[1024,6144]{1,0:T(8,128)(2,1)}, f32[8,128]{1,0:T(8,128)S(1)}) custom-call(f32[32,1,128]{2,1,0:T(1,128)S(1)} %all_to_all.5.parts_ref, bf16[1024,40]{1,0:T(8,128)(2,1)S(1)} %get-tuple-element.43.ht_ref, bf16[8,40,768]{2,1,0:T(8,128)(2,1)S(1)} %bitcast.9, bf16[1024,6144]{1,0:T(8,128)(2,1)S(1)} %get-tuple-element.37.refs_5_.refs_4_.v0_ref, ...), custom_call_target="tpu_custom_call" | custom-call | flops 503316480 | bytes 37748736 | tf_op jit(solution)/shard_map/residual/pallas_call | solution.py:444
  82.7 0.6 copy.10
  (3 shorter events, 0.0 us)
Async XLA Ops:
  0.6 16.4 %collective-permute-start.1 = (bf16[16,6144]{1,0:T(8,128)(2,1)}, bf16[16,6144]{1,0:T(8,128)(2,1)S(1)}, u32[]{:S(2)}, u32[]{:S(2)}) collective-permute-start(bf16[16,6144]{1,0:T(8,128)(2,1)} %refs_0_.1), channel_id=1, source_target_pairs={{0,16},{8,24},{16,0},{24,8},{1,17},{9,25},{17,1},{25,9},{2,18},{10... | collective-permute-start | bytes 589832 | tf_op jit(solution)/shard_map/ppermute | solution.py:473
  3.7 13.4 %collective-permute-start = (bf16[16,6144]{1,0:T(8,128)(2,1)}, bf16[16,6144]{1,0:T(8,128)(2,1)S(1)}, u32[]{:S(2)}, u32[]{:S(2)}) collective-permute-start(bf16[16,6144]{1,0:T(8,128)(2,1)} %refs_0_.1), channel_id=1, source_target_pairs={{0,8},{8,0},{16,24},{24,16},{1,9},{9,1},{17,25},{25,17},{2,10},{10... | collective-permute-start | bytes 589832 | tf_op jit(solution)/shard_map/ppermute | solution.py:473
  5.2 11.9 %collective-permute-start.2 = (bf16[16,6144]{1,0:T(8,128)(2,1)}, bf16[16,6144]{1,0:T(8,128)(2,1)S(1)}, u32[]{:S(2)}, u32[]{:S(2)}) collective-permute-start(bf16[16,6144]{1,0:T(8,128)(2,1)} %refs_0_.1), channel_id=1, source_target_pairs={{0,24},{8,16},{16,8},{24,0},{1,25},{9,17},{17,9},{25,1},{2,26},{10... | collective-permute-start | bytes 589832 | tf_op jit(solution)/shard_map/ppermute | solution.py:473
  5.3 0.7 copy-start.1
  6.1 0.7 copy-start.2
  6.7 0.7 copy-start.3
  7.4 0.7 copy-start.4
  8.1 9.0 %copy-start = (bf16[16,6144]{1,0:T(8,128)(2,1)S(1)}, bf16[16,6144]{1,0:T(8,128)(2,1)}, u32[]{:S(2)}) copy-start(bf16[16,6144]{1,0:T(8,128)(2,1)} %refs_0_.1) | copy-start | bytes 589828
  26.2 1.6 %collective-permute-start.3 = (bf16[4,40,768]{2,1,0:T(8,128)(2,1)S(1)}, bf16[4,40,768]{2,1,0:T(8,128)(2,1)S(1)}, u32[]{:S(2)}, u32[]{:S(2)}) collective-permute-start(bf16[4,40,768]{2,1,0:T(8,128)(2,1)S(1)} %get-tuple-element.30.refs_1_), channel_id=1, source_target_pairs={{0,1},{1,0},{2,3},{3,2},{4,5},{5,4},{6,7},{7,6},{8,9},{9,8},{10,11... | collective-permute-start | bytes 737288 | tf_op jit(solution)/shard_map/ppermute | solution.py:473
  27.8 11.7 %collective-permute-start.4 = (bf16[40,768]{1,0:T(8,128)(2,1)S(1)}, bf16[40,768]{1,0:T(8,128)(2,1)S(1)}, u32[]{:S(2)}, u32[]{:S(2)}) collective-permute-start(bf16[40,768]{1,0:T(8,128)(2,1)S(1)} %get-tuple-element.34), channel_id=1, source_target_pairs={{0,8},{8,0},{16,24},{24,16},{1,9},{9,1},{17,25},{25,17},{2,10},{10... | collective-permute-start | bytes 184328 | tf_op jit(solution)/shard_map/ppermute | solution.py:473
  29.8 9.8 %collective-permute-start.5 = (bf16[40,768]{1,0:T(8,128)(2,1)S(1)}, bf16[40,768]{1,0:T(8,128)(2,1)S(1)}, u32[]{:S(2)}, u32[]{:S(2)}) collective-permute-start(bf16[40,768]{1,0:T(8,128)(2,1)S(1)} %get-tuple-element.35), channel_id=1, source_target_pairs={{0,16},{8,24},{16,0},{24,8},{1,17},{9,25},{17,1},{25,9},{2,18},{10... | collective-permute-start | bytes 184328 | tf_op jit(solution)/shard_map/ppermute | solution.py:473
  31.3 8.2 %collective-permute-start.6 = (bf16[40,768]{1,0:T(8,128)(2,1)S(1)}, bf16[40,768]{1,0:T(8,128)(2,1)S(1)}, u32[]{:S(2)}, u32[]{:S(2)}) collective-permute-start(bf16[40,768]{1,0:T(8,128)(2,1)S(1)} %get-tuple-element.36), channel_id=1, source_target_pairs={{0,24},{8,16},{16,8},{24,0},{1,25},{9,17},{17,9},{25,1},{2,26},{10... | collective-permute-start | bytes 184328 | tf_op jit(solution)/shard_map/ppermute | solution.py:473
  39.6 10.2 %collective-permute-start.9 = (bf16[40,768]{1,0:T(8,128)(2,1)S(1)}, bf16[40,768]{1,0:T(8,128)(2,1)S(1)}, u32[]{:S(2)}, u32[]{:S(2)}) collective-permute-start(bf16[40,768]{1,0:T(8,128)(2,1)S(1)} %get-tuple-element.40.refs_0_), channel_id=1, source_target_pairs={{0,6},{2,4},{4,2},{6,0},{1,7},{3,5},{5,3},{7,1},{8,14},{10,12},{12... | collective-permute-start | bytes 184328 | tf_op jit(solution)/shard_map/ppermute | solution.py:473
  43.7 6.1 %collective-permute-start.8 = (bf16[40,768]{1,0:T(8,128)(2,1)S(1)}, bf16[40,768]{1,0:T(8,128)(2,1)S(1)}, u32[]{:S(2)}, u32[]{:S(2)}) collective-permute-start(bf16[40,768]{1,0:T(8,128)(2,1)S(1)} %get-tuple-element.40.refs_0_), channel_id=1, source_target_pairs={{0,4},{2,6},{4,0},{6,2},{1,5},{3,7},{5,1},{7,3},{8,12},{10,14},{12... | collective-permute-start | bytes 184328 | tf_op jit(solution)/shard_map/ppermute | solution.py:473
  43.7 6.1 %collective-permute-start.7 = (bf16[40,768]{1,0:T(8,128)(2,1)S(1)}, bf16[40,768]{1,0:T(8,128)(2,1)S(1)}, u32[]{:S(2)}, u32[]{:S(2)}) collective-permute-start(bf16[40,768]{1,0:T(8,128)(2,1)S(1)} %get-tuple-element.40.refs_0_), channel_id=1, source_target_pairs={{0,2},{2,0},{4,6},{6,4},{1,3},{3,1},{5,7},{7,5},{8,10},{10,8},{12,... | collective-permute-start | bytes 184328 | tf_op jit(solution)/shard_map/ppermute | solution.py:473

commit v3 on v2

--- a/solution.py
+++ b/solution.py
@@ -16,7 +16,6 @@
 MIB = 1 << 20
 F32 = jnp.float32
 BF16 = jnp.bfloat16
-PLANE = ("dp", "slice")
 EVERY = ("dp", "group", "slice")
 
 
@@ -40,18 +39,28 @@
     return best
 
 
-def load_kernel(tok_dev, ids_ref, routes_ref, gates_ref, rho_ref, sigma_ref, wg_hbm, wu_hbm, *outs):
-    wg_ref, wu_ref, place_ref, gate_ref, rho_row_ref, sigma_row_ref, sems = outs
+def load_kernel(tok_dev, ids_ref, routes_hbm, gates_hbm, rho_hbm, sigma_hbm, wg_hbm, wu_hbm, *outs):
+    wg_ref, wu_ref, place_ref, gate_ref, rho_row_ref, sigma_row_ref = outs[:6]
+    routes_ref, gates_ref, rho_ref, small_sems, w_sems = outs[6:]
     source, group, chunk = ids_ref[0], ids_ref[1], ids_ref[2]
-    blocks = sems.shape[1]
-    depth = wg_ref.shape[0] // blocks
-    copies = []
-    for i in range(blocks):
+    wide = rho_row_ref.shape[1]
+    here = pl.ds(pl.multiple_of(chunk * wide, 128), wide)
+    small = [
+        pltpu.make_async_copy(routes_hbm, routes_ref, small_sems.at[0]),
+        pltpu.make_async_copy(gates_hbm, gates_ref, small_sems.at[1]),
+        pltpu.make_async_copy(rho_hbm, rho_ref, small_sems.at[2]),
+        pltpu.make_async_copy(sigma_hbm.at[:, here], sigma_row_ref, small_sems.at[3]),
+    ]
+    depth = wg_ref.shape[0] // w_sems.shape[1]
+    weights = []
+    for i in range(w_sems.shape[1]):
         at = pl.ds(i * depth, depth)
-        copies.append(pltpu.make_async_copy(wg_hbm.at[at], wg_ref.at[at], sems.at[0, i]))
-        copies.append(pltpu.make_async_copy(wu_hbm.at[at], wu_ref.at[at], sems.at[1, i]))
-    for copy in copies:
+        weights.append(pltpu.make_async_copy(wg_hbm.at[at], wg_ref.at[at], w_sems.at[0, i]))
+        weights.append(pltpu.make_async_copy(wu_hbm.at[at], wu_ref.at[at], w_sems.at[1, i]))
+    for copy in small + weights:
         copy.start()
+    for copy in small:
+        copy.wait()
 
     experts, rows, total = place_ref.shape
     routes, gates = routes_ref[...], gates_ref[...]
@@ -66,32 +75,29 @@
     start = (lax.broadcasted_iota(jnp.int32, (8, total), 1) // tok_dev) * CAP
     slot = jnp.where(member > 0.0, start + rank, -1)
     row = lax.broadcasted_iota(jnp.int32, (rows, total), 0)
-    places = [(slot[e : e + 1, :] == row).astype(F32).astype(BF16) for e in range(experts)]
     swapped = (first // tok_dev == (second // tok_dev) ^ source) & (first % tok_dev == second % tok_dev)
     for e in range(experts):
-        place_ref[e] = dot(places[e], swapped.astype(F32).astype(BF16)).astype(BF16)
+        place = (slot[e : e + 1, :] == row).astype(F32).astype(BF16)
+        place_ref[e] = dot(place, swapped.astype(F32).astype(BF16)).astype(BF16)
     gate = jnp.zeros((1, total), F32)
     for k in range(routes.shape[0]):
         gate = gate + jnp.where(routes[k : k + 1, :] == group, gates[k : k + 1, :], 0.0)
     gate_ref[...] = jnp.sum(jnp.where(swapped, gate, 0.0), axis=1, keepdims=True)
-    wide = rho_row_ref.shape[1]
     rho_row_ref[...] = jnp.zeros_like(rho_row_ref)
     rho_row_ref[:, 0:tok_dev] = rho_ref[...]
-    sigma_row_ref[...] = sigma_ref[:, pl.ds(pl.multiple_of(chunk * wide, 128), wide)]
-
-    for copy in copies:
+
+    for copy in weights:
         copy.wait()
 
 
 def load_call(ids, routes, gates, rho, sigma, w_gate, w_up, tok_dev, rows, wide):
     features, units = w_gate.shape
     total = routes.shape[1]
-    blocks = features // divisor(features, 128, 1024)
     vmem = pl.BlockSpec(memory_space=pltpu.VMEM)
     hbm = pl.BlockSpec(memory_space=pltpu.HBM)
     return pl.pallas_call(
         functools.partial(load_kernel, tok_dev),
-        in_specs=[pl.BlockSpec(memory_space=pltpu.SMEM), vmem, vmem, vmem, vmem, hbm, hbm],
+        in_specs=[pl.BlockSpec(memory_space=pltpu.SMEM)] + [hbm] * 6,
         out_specs=[vmem] * 6,
         out_shape=[
             pltpu.VMEM((features, units), BF16),
@@ -101,49 +107,57 @@
             jax.ShapeDtypeStruct((1, wide), F32),
             jax.ShapeDtypeStruct((1, wide), F32),
         ],
-        scratch_shapes=[pltpu.SemaphoreType.DMA((2, blocks))],
+        scratch_shapes=[
+            pltpu.VMEM(routes.shape, jnp.int32),
+            pltpu.VMEM(gates.shape, F32),
+            pltpu.VMEM(rho.shape, F32),
+            pltpu.SemaphoreType.DMA((4,)),
+            pltpu.SemaphoreType.DMA((2, features // divisor(features, 128, 1024))),
+        ],
         compiler_params=params(3),
         cost_estimate=pl.CostEstimate(flops=0, bytes_accessed=8 * features * units, transcendentals=0),
         name="load",
     )(ids, routes, gates, rho, sigma, w_gate, w_up)
 
 
+def vector_blocks(units):
+    return 4 if units % 512 == 0 else 1
+
+
 def hidden_kernel(scale, parts, cuts, column_ref, *refs):
     xs, (wg_ref, wu_ref, gate_ref, place_ref, v_hbm) = refs[:parts], refs[parts : parts + 5]
     outs = refs[parts + 5 :]
     h_ref, v_ref, tangents = outs[0], outs[1], outs[2 : 2 + cuts]
-    acc_g, acc_u, sems = outs[2 + cuts :]
+    acc_g, acc_u, v_sems = outs[2 + cuts :]
     units, features = v_ref.shape
-    blocks = sems.shape[0]
-    copies = []
-    for i in range(blocks):
-        at = pl.ds(i * (units // blocks), units // blocks)
-        copies.append(pltpu.make_async_copy(v_hbm.at[BASIS - 1, at], v_ref.at[at], sems.at[i]))
-    for copy in copies:
+    depth = divisor(features, 128, 1024)
+    lots = [pl.ds(i * depth, depth) for i in range(features // depth)]
+    height = units // v_sems.shape[0]
+    bands = [pl.ds(i * height, height) for i in range(v_sems.shape[0])]
+    vectors = [
+        pltpu.make_async_copy(v_hbm.at[BASIS - 1, at], v_ref.at[at], v_sems.at[i]) for i, at in enumerate(bands)
+    ]
+    for copy in vectors:
         copy.start()
 
-    depth = divisor(features, 128, 1024)
-    for i in range(features // depth):
-        at = pl.ds(i * depth, depth)
-        x = jnp.concatenate([ref[:, at] for ref in xs], axis=0)
-        part_g, part_u = dot(x, wg_ref[at, :]), dot(x, wu_ref[at, :])
-        if i:
-            acc_g[...] += part_g
-            acc_u[...] += part_u
-        else:
-            acc_g[...] = part_g
-            acc_u[...] = part_u
+    def project(acc, w_ref):
+        for i, at in enumerate(lots):
+            part = dot(jnp.concatenate([ref[:, at] for ref in xs], axis=0), w_ref[at, :])
+            acc[...] = acc[...] + part if i else part
+
+    project(acc_g, wg_ref)
+    project(acc_u, wu_ref)
     g = acc_g[...]
     full = (g * (1.0 / (1.0 + jnp.exp(-g))) * acc_u[...] * gate_ref[...]).astype(BF16)
-    h = dot(place_ref[0], full).astype(BF16)
-    h_ref[...] = h
-
-    for copy in copies:
+    h_ref[...] = dot(place_ref[0], full).astype(BF16)
+
+    sources, _, wide = tangents[0].shape
+    for copy in vectors:
         copy.wait()
-    wide = tangents[0].shape[2]
+    h = h_ref[...]
     for j, out_ref in enumerate(tangents):
-        for d in range(out_ref.shape[0]):
-            start = pl.multiple_of(column_ref[j * out_ref.shape[0] + d] * wide, 128)
+        for d in range(sources):
+            start = pl.multiple_of(column_ref[j * sources + d] * wide, 128)
             out_ref[d] = (dot(h, v_ref[:, pl.ds(start, wide)]) * scale).astype(out_ref.dtype)
 
 
@@ -152,10 +166,8 @@
     _, rows, total = place.shape
     sources = len(xs)
     wide = features // (cuts * sources)
-    blocks = 4 if units % 64 == 0 else 1
     vmem = pl.BlockSpec(memory_space=pltpu.VMEM)
     hbm = pl.BlockSpec(memory_space=pltpu.HBM)
-    wg, wu = pinned(wg, wu)
     return pl.pallas_call(
         functools.partial(hidden_kernel, scale, sources, cuts),
         in_specs=[pl.BlockSpec(memory_space=pltpu.SMEM)] + [vmem] * (sources + 4) + [hbm],
@@ -165,13 +177,17 @@
             pltpu.VMEM((units, features), BF16),
         ]
         + [jax.ShapeDtypeStruct((sources, rows, wide), BF16 if j else F32) for j in range(cuts)],
-        scratch_shapes=[pltpu.VMEM((total, units), F32)] * 2 + [pltpu.SemaphoreType.DMA((blocks,))],
+        scratch_shapes=[
+            pltpu.VMEM((total, units), F32),
+            pltpu.VMEM((total, units), F32),
+            pltpu.SemaphoreType.DMA((vector_blocks(units),)),
+        ],
         compiler_params=params(8),
         cost_estimate=pl.CostEstimate(
             flops=6 * rows * features * units, bytes_accessed=6 * features * units, transcendentals=0
         ),
         name="hidden",
-    )(column, *xs, wg, wu, gate, place, basis)
+    )(column, *xs, *pinned(wg, wu), gate, place, basis)
 
 
 def products_of(pairs, reads, units, features):
@@ -250,25 +266,24 @@
     )(hidden, basis, after, *pinned(held))
 
 
-def gram_kernel(v0_ref, v1_ref, after_ref, out_ref):
-    units, features = v0_ref.shape
-    out_ref[0], out_ref[1] = products_of(((0, 1), (1, 1)), (v0_ref, v1_ref), units, features)
-
-
-def gram_call(v0, v1, after):
+def gram_kernel(first, last, v0_ref, v1_ref, after_ref, out_ref):
+    at = pl.ds(first, last - first)
+    reads = (v0_ref.at[at], v1_ref.at[at])
+    out_ref[0], out_ref[1] = products_of(((0, 1), (1, 1)), reads, last - first, v0_ref.shape[1])
+
+
+def gram_call(v0, v1, after, first, last):
     vmem = pl.BlockSpec(memory_space=pltpu.VMEM)
-    v0, v1 = pinned(v0, v1)
-    return pl.pallas_call(
-        gram_kernel,
+    size = (last - first) * v0.shape[1]
+    return pl.pallas_call(
+        functools.partial(gram_kernel, first, last),
         in_specs=[vmem, vmem, pl.BlockSpec(memory_space=pltpu.HBM)],
         out_specs=vmem,
         out_shape=jax.ShapeDtypeStruct((2, 8, 256), F32),
         compiler_params=params(2),
-        cost_estimate=pl.CostEstimate(
-            flops=4 * v0.shape[0] * v0.shape[1], bytes_accessed=4 * v0.shape[0] * v0.shape[1], transcendentals=0
-        ),
+        cost_estimate=pl.CostEstimate(flops=4 * size, bytes_accessed=4 * size, transcendentals=0),
         name="gram",
-    )(v0, v1, after)
+    )(*pinned(v0, v1), after)
 
 
 def pieces(x):
@@ -300,11 +315,11 @@
         out_shape=[jax.ShapeDtypeStruct((rows, wide), BF16 if j else F32) for j in range(sources)],
         compiler_params=params(6),
         name="slice_sum",
-    )(*parts, rho_row, *pinned(held))
+    )(*parts, rho_row, *pinned(*held))
 
 
 def sum_kernel(line, *refs):
-    ins, rho_own, out_ref, rho_ref = refs[:-5], refs[-5], refs[-2], refs[-1]
+    ins, rho_own, out_ref, rho_ref = refs[:-6], refs[-6], refs[-2], refs[-1]
     total = ins[0][...]
     rho_ref[0:1, :] = rho_own[:, 0:128]
     for j, ref in enumerate(ins[1:]):
@@ -317,18 +332,18 @@
     out_ref[...] = jnp.where(row < line, total, 0.0).astype(BF16)
 
 
-def sum_call(parts, rho_row, line, held):
+def sum_call(parts, rho_row, line, held, after):
     rows, wide = parts[0].shape
     return pl.pallas_call(
         functools.partial(sum_kernel, line),
-        in_specs=[pl.BlockSpec(memory_space=pltpu.VMEM)] * (len(parts) + 3),
+        in_specs=[pl.BlockSpec(memory_space=pltpu.VMEM)] * (len(parts) + 4),
         out_shape=[
             jax.ShapeDtypeStruct((rows, wide), BF16),
             jax.ShapeDtypeStruct((len(parts), 128), F32),
         ],
         compiler_params=params(6),
         name="plane_sum",
-    )(*parts, rho_row, *pinned(*held))
+    )(*parts, rho_row, *pinned(*held), after)
 
 
 def cotangent_kernel(parts, kappa, place_ref, rho_ref, sigma_ref, *refs):
@@ -349,41 +364,55 @@
     out_ref[...] = dot(place_ref[0], cot).astype(BF16)
 
 
-def cotangent_call(parts, placing, rho_all, sigma_row, kappa, held):
+def cotangent_call(parts, placing, rho_all, sigma_row, kappa, held, after):
     return pl.pallas_call(
         functools.partial(cotangent_kernel, len(parts), kappa),
-        in_specs=[pl.BlockSpec(memory_space=pltpu.VMEM)] * (len(parts) + 5),
+        in_specs=[pl.BlockSpec(memory_space=pltpu.VMEM)] * (len(parts) + 6),
         out_shape=jax.ShapeDtypeStruct(parts[0].shape, BF16),
         compiler_params=params(6),
         name="cotangent",
-    )(placing, rho_all, sigma_row, *parts, *pinned(*held))
-
-
-def products_kernel(scale, column_ref, h_ref, c_ref, t0_ref, square_ref, gram_ref, *refs):
-    tangents, out_ref = refs[:-1], refs[-1]
-    rows = c_ref.shape[1]
+    )(placing, rho_all, sigma_row, *parts, *pinned(*held), after)
+
+
+def stack_kernel(*refs):
+    for j, ref in enumerate(refs[:-2]):
+        refs[-1][j] = ref[...]
+
+
+def stack_call(parts, after):
+    return pl.pallas_call(
+        stack_kernel,
+        in_specs=[pl.BlockSpec(memory_space=pltpu.VMEM)] * (len(parts) + 1),
+        out_specs=pl.BlockSpec(memory_space=pltpu.VMEM),
+        out_shape=jax.ShapeDtypeStruct((len(parts),) + parts[0].shape, parts[0].dtype),
+        compiler_params=params(6),
+        name="stack",
+    )(*parts, after)
+
+
+def products_kernel(scale, cuts, column_ref, h_ref, t0_ref, square_ref, *refs):
+    out_ref = refs[-1]
+    cots, tangents, grams = refs[:cuts], refs[cuts : 2 * cuts], refs[2 * cuts : -1]
+    sources, rows, wide = cots[0].shape
     h = h_ref[...]
     weight = dot(h, h, ((1,), (1,)))
-    c0 = jnp.zeros(c_ref.shape[1:], F32)
-    c1 = jnp.zeros(c_ref.shape[1:], F32)
+    c0 = jnp.zeros((rows, wide), F32)
+    c1 = jnp.zeros((rows, wide), F32)
     square = jnp.zeros((rows, rows), F32)
-    place = 0
-    for t_ref in tangents:
-        for d in range(t_ref.shape[0]):
-            c = column_ref[place]
-            place += 1
-            cot = c_ref[c]
-            wide = cot.astype(F32)
-            c0 = c0 + wide * t0_ref[c].astype(F32)
-            c1 = c1 + wide * t_ref[d].astype(F32)
+    for j in range(cuts):
+        for d in range(sources):
+            cot = cots[j][d]
+            value = cot.astype(F32)
+            c0 = c0 + value * t0_ref[column_ref[j * sources + d]].astype(F32)
+            c1 = c1 + value * tangents[j][d].astype(F32)
             square = square + dot(cot, cot, ((1,), (1,)))
     values = (
         jnp.sum(c0),
         jnp.sum(c1),
         jnp.sum(weight * square) * (scale * scale),
         jnp.sum(square_ref[...]),
-        jnp.sum(gram_ref[0]),
-        jnp.sum(gram_ref[1]),
+        jnp.sum(sum(ref[0] for ref in grams)),
+        jnp.sum(sum(ref[1] for ref in grams)),
     )
     lane = lax.broadcasted_iota(jnp.int32, out_ref.shape, 2)
     out = jnp.zeros(out_ref.shape, F32)
@@ -392,43 +421,48 @@
     out_ref[...] = out
 
 
-def products_call(column, hidden, cot, t0, square, gram, tangents, scale, devices, held):
+def products_call(column, hidden, t0, square, cots, tangents, grams, scale, devices):
     vmem = pl.BlockSpec(memory_space=pltpu.VMEM)
-    return pl.pallas_call(
-        functools.partial(products_kernel, scale),
-        in_specs=[pl.BlockSpec(memory_space=pltpu.SMEM)] + [vmem] * (5 + len(tangents) + len(held)),
+    args = (hidden, t0, square, *cots, *tangents, *grams)
+    return pl.pallas_call(
+        functools.partial(products_kernel, scale, len(cots)),
+        in_specs=[pl.BlockSpec(memory_space=pltpu.SMEM)] + [vmem] * len(args),
         out_specs=vmem,
         out_shape=jax.ShapeDtypeStruct((devices, 1, 128), F32),
         compiler_params=params(8),
         name="products",
-    )(column, hidden, cot, t0, square, gram, *tangents, *pinned(*held))
-
-
-def final_kernel(scale, entries, parts_ref, ht_ref, c_ref, v0_ref, v1_ref, out_ref, hess_ref, scalars):
-    units, wide = out_ref.shape
-
-    @pl.when(pl.program_id(0) == 0)
+    )(column, *args)
+
+
+def final_kernel(scale, entries, sources, column_ref, parts_ref, ht_ref, v0_ref, v1_ref, *refs):
+    cots, (out_ref, hess_ref, scalars) = refs[:-3], refs[-3:]
+    step = pl.program_id(0)
+
+    @pl.when(step == 0)
     def _():
         total = jnp.sum(parts_ref[...], axis=0) * (1.0 / entries)
         c0, c1, square = total[:, 0:1], total[:, 1:2], total[:, 2:3]
         g00, g01, g11 = total[:, 3:4], total[:, 4:5], total[:, 5:6]
         norm = square - 2.0 * (c0 * c0 + c1 * c1) + c0 * c0 * g00 + 2.0 * c0 * c1 * g01 + c1 * c1 * g11
         beta = jnp.sqrt(jnp.maximum(norm, square * 2.0**-24))
-        line = lax.broadcasted_iota(jnp.int32, (8, 128), 0)
-        hess_ref[...] = jnp.where(line == 0, c0, jnp.where(line == 1, c1, beta))
+        lane = lax.broadcasted_iota(jnp.int32, hess_ref.shape, 1)
+        hess_ref[...] = jnp.where(lane == 0, c0, jnp.where(lane == 1, c1, beta))
         inverse = 1.0 / beta
         scalars[0] = (c0 * inverse)[0, 0]
         scalars[1] = (c1 * inverse)[0, 0]
         scalars[2] = (scale * inverse)[0, 0]
 
     a0, a1, s = scalars[0], scalars[1], scalars[2]
+    units, wide = out_ref.shape
     strip = 256 if units % 256 == 0 else units
     across = divisor(wide, 128, 256)
-    begin = pl.program_id(0) * wide
+    begin = column_ref[step] * wide
     for q in range(wide // across):
         source = pl.ds(pl.multiple_of(begin + q * across, 128), across)
         target = pl.ds(q * across, across)
-        cot = c_ref[0, :, target]
+        cot = cots[0][0, :, target]
+        for j, ref in enumerate(cots[1:]):
+            cot = jnp.where(step // sources == j + 1, ref[0, :, target], cot)
         for i in range(units // strip):
             at = pl.ds(i * strip, strip)
             image = dot(ht_ref[at, :], cot)
@@ -436,36 +470,39 @@
             out_ref[at, target] = out.astype(BF16)
 
 
-def final_call(parts, hidden_t, cot, v0, v1, scale, entries):
+def final_call(column, parts, hidden_t, cots, v0, v1, scale, entries):
     units, rows = hidden_t.shape
-    chunks, _, wide = cot.shape
+    sources, _, wide = cots[0].shape
+    features = v0.shape[1]
     vmem = pl.BlockSpec(memory_space=pltpu.VMEM)
-    v0, v1 = pinned(v0, v1)
-    return pl.pallas_call(
-        functools.partial(final_kernel, scale, entries),
-        grid=(chunks,),
-        in_specs=[
-            pl.BlockSpec(parts.shape, lambda c: (0, 0, 0)),
-            pl.BlockSpec((units, rows), lambda c: (0, 0)),
-            pl.BlockSpec((1, rows, wide), lambda c: (c, 0, 0)),
-            vmem,
-            vmem,
+    return pl.pallas_call(
+        functools.partial(final_kernel, scale, entries, sources),
+        grid_spec=pltpu.PrefetchScalarGridSpec(
+            num_scalar_prefetch=1,
+            grid=(len(cots) * sources,),
+            in_specs=[
+                pl.BlockSpec(parts.shape, lambda c, column: (0, 0, 0)),
+                pl.BlockSpec((units, rows), lambda c, column: (0, 0)),
+                vmem,
+                vmem,
+            ]
+            + [pl.BlockSpec((1, rows, wide), lambda c, column: (c % sources, 0, 0))] * len(cots),
+            out_specs=[
+                pl.BlockSpec((units, wide), lambda c, column: (0, column[c])),
+                pl.BlockSpec((1, BASIS + 1), lambda c, column: (0, 0)),
+            ],
+            scratch_shapes=[pltpu.SMEM((4,), F32)],
+        ),
+        out_shape=[
+            jax.ShapeDtypeStruct((units, features), BF16),
+            jax.ShapeDtypeStruct((1, BASIS + 1), F32),
         ],
-        out_specs=[
-            pl.BlockSpec((units, wide), lambda c: (0, c)),
-            pl.BlockSpec((8, 128), lambda c: (0, 0)),
-        ],
-        out_shape=[
-            jax.ShapeDtypeStruct((units, chunks * wide), BF16),
-            jax.ShapeDtypeStruct((8, 128), F32),
-        ],
-        scratch_shapes=[pltpu.SMEM((4,), F32)],
         compiler_params=params(8),
         cost_estimate=pl.CostEstimate(
-            flops=2 * rows * units * chunks * wide, bytes_accessed=6 * units * chunks * wide, transcendentals=0
+            flops=2 * rows * units * features, bytes_accessed=6 * units * features, transcendentals=0
         ),
         name="residual",
-    )(parts, hidden_t, cot, v0, v1)
+    )(column, parts, hidden_t, *pinned(v0, v1), *cots)
 
 
 def swap(x, axis, distance):
@@ -491,31 +528,36 @@
     lane = part if split else 0
     column = ((place % sources) ^ source) * cuts + ((place // sources) ^ lane)
     ids = jnp.stack([source, group, column[0]]).astype(jnp.int32)
-    w_gate, w_up, basis = (pltpu.with_memory_space_constraint(x, pltpu.HBM) for x in (w_gate, w_up, basis))
+    hbm = functools.partial(pltpu.with_memory_space_constraint, memory_space=pltpu.HBM)
+    w_gate, w_up, basis = hbm(w_gate), hbm(w_up), hbm(basis)
 
     xs = [tokens] + [swap(tokens, "dp", j) for j in range(1, sources)]
-    wg, wu, placing, gate, rho_row, sigma_row = load_call(
-        ids, routes.T, gates.T, rho[None, :], sigma[None, :], w_gate, w_up, tok_dev, rows, wide
-    )
+    small = hbm(routes.T), hbm(gates.T), hbm(rho[None, :]), hbm(sigma[None, :])
+    wg, wu, placing, gate, rho_row, sigma_row = load_call(ids, *small, w_gate, w_up, tok_dev, rows, wide)
     hidden, v1, *tangents = hidden_call(column, xs, wg, wu, gate, placing, basis, cuts, scale)
     if split:
         got = [tangents[0]] + [swap(tangents[j], "slice", j) for j in range(1, slices)]
     else:
         got = [lax.psum(tangents[0], "slice")]
-    shares = share_call(got, rho_row, line, v1)
+    shares = share_call(got, rho_row, line, (v1,))
     got = [shares[0]] + [swap(shares[j], "dp", j) for j in range(1, sources)]
     v0, t0, hidden_t, square = other_call(hidden, basis, shares[0], v1, chunks, scale)
-    summed, rho_all = sum_call(got, rho_row, line, (v0, v1))
+    summed, rho_all = sum_call(got, rho_row, line, (v0, v1), hidden_t)
     got = [summed] + [swap(summed, "group", j) for j in range(1, E)]
-    gram = gram_call(v0, v1, rho_all)
-    cot = cotangent_call(got, placing, rho_all, sigma_row, kappa, (v0, v1))
-    cot = lax.all_gather(cot, PLANE if split else "dp", axis=0)
+    units = v0.shape[0]
+    cut = units // 4 * 3
+    grams = [gram_call(v0, v1, rho_all, 0, cut)]
+    cot = cotangent_call(got, placing, rho_all, sigma_row, kappa, (v0, v1), grams[0])
+    cots = [cot] + [swap(cot, "dp", j) for j in range(1, sources)]
+    grams.append(gram_call(v0, v1, cot, cut, units))
+    cots = stack_call(cots, grams[1])
+    cots = [cots] + ([swap(cots, "slice", j) for j in range(1, slices)] if split else [])
 
     devices = sources * E * slices
-    parts = products_call(column, hidden, cot, t0, square, gram, tangents, scale, devices, ())
+    parts = products_call(column, hidden, t0, square, cots, tangents, grams, scale, devices)
     parts = lax.all_to_all(parts, EVERY, 0, 0, tiled=True)
-    new, hess = final_call(parts, hidden_t, cot, v0, v1, scale, entries)
-    return new, hess[: BASIS + 1, :1]
+    new, hess = final_call(column, parts, hidden_t, cots, v0, v1, scale, entries)
+    return new, hess.T
 
 
 def solution(mesh):

time: 83.6 us -> 78.6 us (0.940)
  blocking collectives: 21.9 us -> 11.7 us
  waiting for transfers between devices: 1.52 us -> 5.64 us
  starting transfers between devices: 12.9 us -> 16.6 us
  local copies, waits for them, and re-layouts: 3.35 us -> 0.01 us
  Pallas kernels: 42.7 us -> 43.6 us
    all_gather x1 -> x0, blocking collectives: 10 us -> none  [body(): cot = lax.all_gather(cot, PLANE if split else 'dp', axis=0)]
    ppermute x10 -> x14, waiting for transfers between devices: 1.52 us -> 5.64 us  [swap(): return lax.ppermute(x, axis, [(i, i ^ distance) for i in range(size)])]
    ppermute x10 -> x14, starting transfers between devices: 12.9 us -> 16.6 us  [swap(): return lax.ppermute(x, axis, [(i, i ^ distance) for i in range(size)])]
    unnamed x11 -> x2, local copies, waits for them, and re-layouts: 3.35 us -> 0.01 us
    pallas_call x3 -> x5, Pallas kernels: 16 us -> 16.8 us  [the longest x1 10.2 us: final_call(): pl.pallas_call(functools.partial(final_kernel, scale, entries, sources),...]
  transfers between devices with their start and end apart: 10 -> 14, of which waited for: 1 -> 6; matrix products, arithmetic and copies ran while one was open for 0% -> 0% of each run, Pallas kernels for 27% -> 29%
where the time goes in v3:
time: 78.6 us; the launch traced here: 78.4 us
  Pallas kernels  43.6 us (55%)
  starting transfers between devices  16.6 us (21%)
  blocking collectives  11.7 us (15%)
  waiting for transfers between devices  5.64 us (7%)
  between operations  0.79 us (1%)
    ppermute x14, starting transfers between devices, swap(): return lax.ppermute(x, axis, [(i, i ^ distance) for i in range(size)])  16.6 us
    all_to_all x1, blocking collectives, body(): parts = lax.all_to_all(parts, EVERY, 0, 0, tiled=True)  11.7 us
    pallas_call x1, Pallas kernels, final_call(): pl.pallas_call(functools.partial(final_kernel, scale, entries, sources),...  10.2 us
    pallas_call x1, Pallas kernels, hidden_call(): pl.pallas_call(functools.partial(hidden_kernel, scale, sources, cuts), in...  9.17 us
    pallas_call x1, Pallas kernels, load_call(): pl.pallas_call(functools.partial(load_kernel, tok_dev), in_specs=[pl.Bloc...  8.93 us
    pallas_call x1, Pallas kernels, other_call(): pl.pallas_call(functools.partial(other_kernel, scale), in_specs=[vmem, hb...  8.16 us
    ppermute x14, waiting for transfers between devices, swap(): return lax.ppermute(x, axis, [(i, i ^ distance) for i in range(size)])  5.64 us
    pallas_call x2, Pallas kernels, gram_call(): pl.pallas_call(functools.partial(gram_kernel, first, last), in_specs=[vme...  5.55 us
  transfers between devices with their start and end apart: 14, of which 6 were waited for; matrix products, arithmetic and copies ran while one was open for 0% of the time, Pallas kernels for 29%

profile of v3, /device:TPU:0, one launch (start us, length us, event | category | flops | bytes accessed | tf_op | source)
XLA Modules:
  0.0 78.4 jit_solution(8957371537001469546)
XLA Ops:
  0.6 3.0 %collective-permute-start.1 = (bf16[16,6144]{1,0:T(8,128)(2,1)}, bf16[16,6144]{1,0:T(8,128)(2,1)S(1)}, u32[]{:S(2)}, u32[]{:S(2)}) collective-permute-start(bf16[16,6144]{1,0:T(8,128)(2,1)} %refs_0_.1), channel_id=1, source_target_pairs={{0,16},{8,24},{16,0},{24,8},{1,17},{9,25},{17,1},{25,9},{2,18},{10... | collective-permute-start | bytes 589832 | tf_op jit(solution)/shard_map/ppermute | solution.py:510
  3.7 1.5 %collective-permute-start = (bf16[16,6144]{1,0:T(8,128)(2,1)}, bf16[16,6144]{1,0:T(8,128)(2,1)S(1)}, u32[]{:S(2)}, u32[]{:S(2)}) collective-permute-start(bf16[16,6144]{1,0:T(8,128)(2,1)} %refs_0_.1), channel_id=1, source_target_pairs={{0,8},{8,0},{16,24},{24,16},{1,9},{9,1},{17,25},{25,17},{2,10},{10... | collective-permute-start | bytes 589832 | tf_op jit(solution)/shard_map/ppermute | solution.py:510
  5.2 0.1 collective-permute-start.2
  5.2 0.1 pad_add_fusion.ids_ref
  5.3 0.0 copy-start
  5.3 8.9 %load.1 = (bf16[6144,1024]{1,0:T(8,128)(2,1)S(1)}, bf16[6144,1024]{1,0:T(8,128)(2,1)S(1)}, bf16[4,40,64]{2,1,0:T(8,128)(2,1)S(1)}, f32[64,1]{1,0:T(8,128)S(1)}, ...) custom-call(s32[3]{0:T(128)S(1)} %pad_add_fusion.ids_ref, s32[2,64]{1,0:T(2,128)} %bitcast.10, f32[2,64]{1,0:T(2,128)} %bitcast.11, ...), custom_call_target="tpu_custom_call" | custom-call | bytes 50331648 | tf_op jit(solution)/shard_map/load/pallas_call | solution.py:98
  14.3 0.0 collective-permute-done.1.refs_2_
  14.3 0.0 collective-permute-done.refs_1_
  14.3 0.0 collective-permute-done.2.refs_3_
  14.3 0.0 copy-done
  14.3 9.2 %hidden.1 = (bf16[40,1024]{1,0:T(8,128)(2,1)S(1)}, bf16[1024,6144]{1,0:T(8,128)(2,1)S(1)}, f32[4,40,768]{2,1,0:T(8,128)S(1)}, bf16[4,40,768]{2,1,0:T(8,128)(2,1)S(1)}) custom-call(s32[8]{0:T(128)S(1)} %fusion.2.column_ref, bf16[16,6144]{1,0:T(8,128)(2,1)S(1)} %copy-done, bf16[16,6144]{1,0:T(8,128)(2,1)S(1)} %collective-permute-done.refs_1_, ...), custom_call_target="tpu_custom_call" | custom-call | flops 1509949440 | bytes 37748736 | tf_op jit(solution)/shard_map/hidden/pallas_call | solution.py:171
  23.5 0.1 collective-permute-start.3
  23.6 1.5 %collective-permute-done.3.refs_1_ = bf16[4,40,768]{2,1,0:T(8,128)(2,1)S(1)} collective-permute-done((bf16[4,40,768]{2,1,0:T(8,128)(2,1)S(1)}, bf16[4,40,768]{2,1,0:T(8,128)(2,1)S(1)}, u32[]{:S(2)}, u32[]{:S(2)}) %collective-permute-start.3) | collective-permute-done | bytes 245792 | tf_op jit(solution)/shard_map/ppermute | solution.py:510
  25.1 0.1 slice_sum.1
  25.1 2.0 %collective-permute-start.4 = (bf16[40,768]{1,0:T(8,128)(2,1)S(1)}, bf16[40,768]{1,0:T(8,128)(2,1)S(1)}, u32[]{:S(2)}, u32[]{:S(2)}) collective-permute-start(bf16[40,768]{1,0:T(8,128)(2,1)S(1)} %get-tuple-element.36), channel_id=1, source_target_pairs={{0,8},{8,0},{16,24},{24,16},{1,9},{9,1},{17,25},{25,17},{2,10},{10... | collective-permute-start | bytes 184328 | tf_op jit(solution)/shard_map/ppermute | solution.py:510
  27.1 1.5 %collective-permute-start.5 = (bf16[40,768]{1,0:T(8,128)(2,1)S(1)}, bf16[40,768]{1,0:T(8,128)(2,1)S(1)}, u32[]{:S(2)}, u32[]{:S(2)}) collective-permute-start(bf16[40,768]{1,0:T(8,128)(2,1)S(1)} %get-tuple-element.37), channel_id=1, source_target_pairs={{0,16},{8,24},{16,0},{24,8},{1,17},{9,25},{17,1},{25,9},{2,18},{10... | collective-permute-start | bytes 184328 | tf_op jit(solution)/shard_map/ppermute | solution.py:510
  28.6 0.0 collective-permute-start.6
  28.7 8.2 %other_tangent.1 = (bf16[1024,6144]{1,0:T(8,128)(2,1)S(1)}, bf16[8,40,768]{2,1,0:T(8,128)(2,1)S(1)}, bf16[1024,40]{1,0:T(8,128)(2,1)S(1)}, f32[8,256]{1,0:T(8,128)S(1)}) custom-call(bf16[40,1024]{1,0:T(8,128)(2,1)S(1)} %get-tuple-element.28.h_ref, bf16[2,1024,6144]{2,1,0:T(8,128)(2,1)} %v_hbm.1, f32[40,768]{1,0:T(8,128)S(1)} %get-tuple-element.33.after_ref.refs_0_, ...), custom_call_target="tpu_custom_call" | custom-call | flops 503316480 | bytes 12582912 | tf_op jit(solution)/shard_map/other_tangent/pallas_call | solution.py:250
  36.9 0.0 collective-permute-done.4.refs_1_
  36.9 0.0 collective-permute-done.5.refs_2_
  36.9 0.0 collective-permute-done.6.refs_3_
  36.9 4.1 %collective-permute-start.9 = (bf16[40,768]{1,0:T(8,128)(2,1)S(1)}, bf16[40,768]{1,0:T(8,128)(2,1)S(1)}, u32[]{:S(2)}, u32[]{:S(2)}) collective-permute-start(bf16[40,768]{1,0:T(8,128)(2,1)S(1)} %get-tuple-element.43.refs_0_), channel_id=1, source_target_pairs={{0,6},{2,4},{4,2},{6,0},{1,7},{3,5},{5,3},{7,1},{8,14},{10,12},{12... | collective-permute-start | bytes 184328 | tf_op jit(solution)/shard_map/ppermute | solution.py:510
  41.0 0.0 collective-permute-start.8
  41.0 0.6 collective-permute-start.7
  41.7 4.1 %gram.2.refs_6_.refs_4_ = f32[2,8,256]{2,1,0:T(8,128)S(1)} custom-call(bf16[1024,6144]{1,0:T(8,128)(2,1)S(1)} %get-tuple-element.39.refs_5_.v0_ref.refs_4_, bf16[1024,6144]{1,0:T(8,128)(2,1)S(1)} %get-tuple-element.32.refs_3_.held_ref.refs_6_.v1_ref.refs_5_, f32[4,128]{1,0:T(4,128)S(1)} %get-tuple-element.41.after_ref.rho_ref), custom_call_target="tpu_custom_call" | custom-call | flops 18874368 | bytes 18874368 | tf_op jit(solution)/shard_map/gram/pallas_call | solution.py:278
  45.8 0.0 collective-permute-done.9.refs_3_
  45.8 0.4 collective-permute-done.8.refs_2_
  46.2 0.0 collective-permute-done.7.refs_1_
  46.2 0.4 cotangent.1.after_ref.refs_0_
  46.6 2.5 %collective-permute-start.12 = (bf16[40,768]{1,0:T(8,128)(2,1)S(1)}, bf16[40,768]{1,0:T(8,128)(2,1)S(1)}, u32[]{:S(2)}, u32[]{:S(2)}) collective-permute-start(bf16[40,768]{1,0:T(8,128)(2,1)S(1)} %cotangent.1.after_ref.refs_0_), channel_id=1, source_target_pairs={{0,24},{8,16},{16,8},{24,0},{1,25},{9,17},{17,9},{25,1},{2,26},{10... | collective-permute-start | bytes 184328 | tf_op jit(solution)/shard_map/ppermute | solution.py:510
  49.1 0.5 collective-permute-start.11
  49.6 0.5 collective-permute-start.10
  50.2 1.4 %gram.3.refs_4_.refs_5_ = f32[2,8,256]{2,1,0:T(8,128)S(1)} custom-call(bf16[1024,6144]{1,0:T(8,128)(2,1)S(1)} %get-tuple-element.39.refs_5_.v0_ref.refs_4_, bf16[1024,6144]{1,0:T(8,128)(2,1)S(1)} %get-tuple-element.32.refs_3_.held_ref.refs_6_.v1_ref.refs_5_, bf16[40,768]{1,0:T(8,128)(2,1)S(1)} %cotangent.1.after_ref.refs_0_), custom_call_target="tpu_custom_call" | custom-call | flops 6291456 | bytes 6291456 | tf_op jit(solution)/shard_map/gram/pallas_call | solution.py:278
  51.6 0.7 collective-permute-done.12.refs_3_
  52.3 1.1 %collective-permute-done.11.refs_2_ = bf16[40,768]{1,0:T(8,128)(2,1)S(1)} collective-permute-done((bf16[40,768]{1,0:T(8,128)(2,1)S(1)}, bf16[40,768]{1,0:T(8,128)(2,1)S(1)}, u32[]{:S(2)}, u32[]{:S(2)}) %collective-permute-start.11) | collective-permute-done | bytes 61472 | tf_op jit(solution)/shard_map/ppermute | solution.py:510
  53.4 0.5 collective-permute-done.10.refs_1_
  53.9 0.1 collective-permute-start.13
  54.0 1.5 %collective-permute-done.13.refs_1_ = bf16[4,40,768]{2,1,0:T(8,128)(2,1)S(1)} collective-permute-done((bf16[4,40,768]{2,1,0:T(8,128)(2,1)S(1)}, bf16[4,40,768]{2,1,0:T(8,128)(2,1)S(1)}, u32[]{:S(2)}, u32[]{:S(2)}) %collective-permute-start.13) | collective-permute-done | bytes 245792 | tf_op jit(solution)/shard_map/ppermute | solution.py:510
  55.5 1.1 %products.1 = f32[32,1,128]{2,1,0:T(1,128)S(1)} custom-call(s32[8]{0:T(128)S(1)} %fusion.2.column_ref, bf16[40,1024]{1,0:T(8,128)(2,1)S(1)} %get-tuple-element.28.h_ref, bf16[8,40,768]{2,1,0:T(8,128)(2,1)S(1)} %get-tuple-element.34.t0_ref, f32[8,256]{1,0:T(8,128)S(1)} %get-tuple-element.35.square_ref, bf16[4,40,768]{2,1,0:T(8,128)(2,1)S(1)} %stack.13.refs_0_, ...), custom_call_target="tpu_custom_call" | custom-call | tf_op jit(solution)/shard_map/products/pallas_call | solution.py:427
  56.5 11.7 %all_to_all.5.parts_ref = f32[32,1,128]{2,1,0:T(1,128)S(1)} all-to-all(f32[32,1,128]{2,1,0:T(1,128)S(1)} %products.1), channel_id=1, replica_groups=mesh['dp'=4,'group'=4,'slice'=2] {'dp','group','slice'}, dimensions={0} | all-to-all | bytes 32768 | tf_op jit(solution)/shard_map/all_to_all | solution.py:558
  68.2 10.2 %residual.1 = (bf16[1024,6144]{1,0:T(8,128)(2,1)}, f32[1,3]{1,0:T(1,128)}) custom-call(s32[8]{0:T(128)S(1)} %fusion.2.column_ref, f32[32,1,128]{2,1,0:T(1,128)S(1)} %all_to_all.5.parts_ref, bf16[1024,40]{1,0:T(8,128)(2,1)S(1)} %get-tuple-element.40.refs_7_.ht_ref, bf16[1024,6144]{1,0:T(8,128)(2,1)S(1)} %get-tuple-element.39.refs_5_.v0_ref.refs_4_, ...), custom_call_target="tpu_custom_call" | custom-call | flops 503316480 | bytes 37748736 | tf_op jit(solution)/shard_map/residual/pallas_call | solution.py:478
  (3 shorter events, 0.1 us)
Async XLA Ops:
  0.6 13.6 %collective-permute-start.1 = (bf16[16,6144]{1,0:T(8,128)(2,1)}, bf16[16,6144]{1,0:T(8,128)(2,1)S(1)}, u32[]{:S(2)}, u32[]{:S(2)}) collective-permute-start(bf16[16,6144]{1,0:T(8,128)(2,1)} %refs_0_.1), channel_id=1, source_target_pairs={{0,16},{8,24},{16,0},{24,8},{1,17},{9,25},{17,1},{25,9},{2,18},{10... | collective-permute-start | bytes 589832 | tf_op jit(solution)/shard_map/ppermute | solution.py:510
  3.7 10.6 %collective-permute-start = (bf16[16,6144]{1,0:T(8,128)(2,1)}, bf16[16,6144]{1,0:T(8,128)(2,1)S(1)}, u32[]{:S(2)}, u32[]{:S(2)}) collective-permute-start(bf16[16,6144]{1,0:T(8,128)(2,1)} %refs_0_.1), channel_id=1, source_target_pairs={{0,8},{8,0},{16,24},{24,16},{1,9},{9,1},{17,25},{25,17},{2,10},{10... | collective-permute-start | bytes 589832 | tf_op jit(solution)/shard_map/ppermute | solution.py:510
  5.2 9.1 %collective-permute-start.2 = (bf16[16,6144]{1,0:T(8,128)(2,1)}, bf16[16,6144]{1,0:T(8,128)(2,1)S(1)}, u32[]{:S(2)}, u32[]{:S(2)}) collective-permute-start(bf16[16,6144]{1,0:T(8,128)(2,1)} %refs_0_.1), channel_id=1, source_target_pairs={{0,24},{8,16},{16,8},{24,0},{1,25},{9,17},{17,9},{25,1},{2,26},{10... | collective-permute-start | bytes 589832 | tf_op jit(solution)/shard_map/ppermute | solution.py:510
  5.3 9.0 %copy-start = (bf16[16,6144]{1,0:T(8,128)(2,1)S(1)}, bf16[16,6144]{1,0:T(8,128)(2,1)}, u32[]{:S(2)}) copy-start(bf16[16,6144]{1,0:T(8,128)(2,1)} %refs_0_.1) | copy-start | bytes 589828
  23.5 1.6 %collective-permute-start.3 = (bf16[4,40,768]{2,1,0:T(8,128)(2,1)S(1)}, bf16[4,40,768]{2,1,0:T(8,128)(2,1)S(1)}, u32[]{:S(2)}, u32[]{:S(2)}) collective-permute-start(bf16[4,40,768]{2,1,0:T(8,128)(2,1)S(1)} %get-tuple-element.30.refs_3_), channel_id=1, source_target_pairs={{0,1},{1,0},{2,3},{3,2},{4,5},{5,4},{6,7},{7,6},{8,9},{9,8},{10,11... | collective-permute-start | bytes 737288 | tf_op jit(solution)/shard_map/ppermute | solution.py:510
  25.1 11.7 %collective-permute-start.4 = (bf16[40,768]{1,0:T(8,128)(2,1)S(1)}, bf16[40,768]{1,0:T(8,128)(2,1)S(1)}, u32[]{:S(2)}, u32[]{:S(2)}) collective-permute-start(bf16[40,768]{1,0:T(8,128)(2,1)S(1)} %get-tuple-element.36), channel_id=1, source_target_pairs={{0,8},{8,0},{16,24},{24,16},{1,9},{9,1},{17,25},{25,17},{2,10},{10... | collective-permute-start | bytes 184328 | tf_op jit(solution)/shard_map/ppermute | solution.py:510
  27.1 9.8 %collective-permute-start.5 = (bf16[40,768]{1,0:T(8,128)(2,1)S(1)}, bf16[40,768]{1,0:T(8,128)(2,1)S(1)}, u32[]{:S(2)}, u32[]{:S(2)}) collective-permute-start(bf16[40,768]{1,0:T(8,128)(2,1)S(1)} %get-tuple-element.37), channel_id=1, source_target_pairs={{0,16},{8,24},{16,0},{24,8},{1,17},{9,25},{17,1},{25,9},{2,18},{10... | collective-permute-start | bytes 184328 | tf_op jit(solution)/shard_map/ppermute | solution.py:510
  28.6 8.2 %collective-permute-start.6 = (bf16[40,768]{1,0:T(8,128)(2,1)S(1)}, bf16[40,768]{1,0:T(8,128)(2,1)S(1)}, u32[]{:S(2)}, u32[]{:S(2)}) collective-permute-start(bf16[40,768]{1,0:T(8,128)(2,1)S(1)} %get-tuple-element.38), channel_id=1, source_target_pairs={{0,24},{8,16},{16,8},{24,0},{1,25},{9,17},{17,9},{25,1},{2,26},{10... | collective-permute-start | bytes 184328 | tf_op jit(solution)/shard_map/ppermute | solution.py:510
  36.9 8.9 %collective-permute-start.9 = (bf16[40,768]{1,0:T(8,128)(2,1)S(1)}, bf16[40,768]{1,0:T(8,128)(2,1)S(1)}, u32[]{:S(2)}, u32[]{:S(2)}) collective-permute-start(bf16[40,768]{1,0:T(8,128)(2,1)S(1)} %get-tuple-element.43.refs_0_), channel_id=1, source_target_pairs={{0,6},{2,4},{4,2},{6,0},{1,7},{3,5},{5,3},{7,1},{8,14},{10,12},{12... | collective-permute-start | bytes 184328 | tf_op jit(solution)/shard_map/ppermute | solution.py:510
  41.0 5.1 %collective-permute-start.8 = (bf16[40,768]{1,0:T(8,128)(2,1)S(1)}, bf16[40,768]{1,0:T(8,128)(2,1)S(1)}, u32[]{:S(2)}, u32[]{:S(2)}) collective-permute-start(bf16[40,768]{1,0:T(8,128)(2,1)S(1)} %get-tuple-element.43.refs_0_), channel_id=1, source_target_pairs={{0,4},{2,6},{4,0},{6,2},{1,5},{3,7},{5,1},{7,3},{8,12},{10,14},{12... | collective-permute-start | bytes 184328 | tf_op jit(solution)/shard_map/ppermute | solution.py:510
  41.0 5.1 %collective-permute-start.7 = (bf16[40,768]{1,0:T(8,128)(2,1)S(1)}, bf16[40,768]{1,0:T(8,128)(2,1)S(1)}, u32[]{:S(2)}, u32[]{:S(2)}) collective-permute-start(bf16[40,768]{1,0:T(8,128)(2,1)S(1)} %get-tuple-element.43.refs_0_), channel_id=1, source_target_pairs={{0,2},{2,0},{4,6},{6,4},{1,3},{3,1},{5,7},{7,5},{8,10},{10,8},{12,... | collective-permute-start | bytes 184328 | tf_op jit(solution)/shard_map/ppermute | solution.py:510
  46.6 5.7 %collective-permute-start.12 = (bf16[40,768]{1,0:T(8,128)(2,1)S(1)}, bf16[40,768]{1,0:T(8,128)(2,1)S(1)}, u32[]{:S(2)}, u32[]{:S(2)}) collective-permute-start(bf16[40,768]{1,0:T(8,128)(2,1)S(1)} %cotangent.1.after_ref.refs_0_), channel_id=1, source_target_pairs={{0,24},{8,16},{16,8},{24,0},{1,25},{9,17},{17,9},{25,1},{2,26},{10... | collective-permute-start | bytes 184328 | tf_op jit(solution)/shard_map/ppermute | solution.py:510
  49.1 4.2 %collective-permute-start.11 = (bf16[40,768]{1,0:T(8,128)(2,1)S(1)}, bf16[40,768]{1,0:T(8,128)(2,1)S(1)}, u32[]{:S(2)}, u32[]{:S(2)}) collective-permute-start(bf16[40,768]{1,0:T(8,128)(2,1)S(1)} %cotangent.1.after_ref.refs_0_), channel_id=1, source_target_pairs={{0,16},{8,24},{16,0},{24,8},{1,17},{9,25},{17,1},{25,9},{2,18},{10... | collective-permute-start | bytes 184328 | tf_op jit(solution)/shard_map/ppermute | solution.py:510
  49.6 4.2 %collective-permute-start.10 = (bf16[40,768]{1,0:T(8,128)(2,1)S(1)}, bf16[40,768]{1,0:T(8,128)(2,1)S(1)}, u32[]{:S(2)}, u32[]{:S(2)}) collective-permute-start(bf16[40,768]{1,0:T(8,128)(2,1)S(1)} %cotangent.1.after_ref.refs_0_), channel_id=1, source_target_pairs={{0,8},{8,0},{16,24},{24,16},{1,9},{9,1},{17,25},{25,17},{2,10},{10... | collective-permute-start | bytes 184328 | tf_op jit(solution)/shard_map/ppermute | solution.py:510
  53.9 1.6 %collective-permute-start.13 = (bf16[4,40,768]{2,1,0:T(8,128)(2,1)S(1)}, bf16[4,40,768]{2,1,0:T(8,128)(2,1)S(1)}, u32[]{:S(2)}, u32[]{:S(2)}) collective-permute-start(bf16[4,40,768]{2,1,0:T(8,128)(2,1)S(1)} %stack.13.refs_0_), channel_id=1, source_target_pairs={{0,1},{1,0},{2,3},{3,2},{4,5},{5,4},{6,7},{7,6},{8,9},{9,8},{10,11... | collective-permute-start | bytes 737288 | tf_op jit(solution)/shard_map/ppermute | solution.py:510

commit v4 on v3

--- a/solution.py
+++ b/solution.py
@@ -211,7 +211,7 @@
     return lax.fori_loop(0, features // wide, column, (zero,) * len(pairs))
 
 
-def other_kernel(scale, h_ref, v_hbm, after_ref, held_ref, v_ref, t_ref, ht_ref, gram_ref, acc, sems):
+def other_kernel(scale, h_ref, v_hbm, after_ref, held_ref, v_ref, t_ref, ht_ref, acc, sems):
     units, features = v_ref.shape
     blocks = sems.shape[0]
     depth = units // blocks
@@ -223,7 +223,6 @@
         copy.start()
     ht_ref[...] = h_ref[...].astype(F32).T.astype(BF16)
     chunks, _, wide = t_ref.shape
-    sums = None
     for i in range(blocks):
         at = pl.ds(i * depth, depth)
         copies[i].wait()
@@ -236,9 +235,6 @@
                 acc[:, across] = part
             else:
                 t_ref[c] = (part * scale).astype(BF16)
-        (square,) = products_of(((0, 0),), (v_ref.at[at],), depth, features)
-        sums = square if sums is None else sums + square
-    gram_ref[...] = sums
 
 
 def other_call(hidden, basis, after, held, chunks, scale):
@@ -250,12 +246,11 @@
     return pl.pallas_call(
         functools.partial(other_kernel, scale),
         in_specs=[vmem, hbm, hbm, vmem],
-        out_specs=[vmem] * 4,
+        out_specs=[vmem] * 3,
         out_shape=[
             pltpu.VMEM((units, features), BF16),
             jax.ShapeDtypeStruct((chunks, rows, features // chunks), BF16),
             jax.ShapeDtypeStruct((units, rows), BF16),
-            jax.ShapeDtypeStruct((8, 256), F32),
         ],
         scratch_shapes=[pltpu.VMEM((rows, features), F32), pltpu.SemaphoreType.DMA((blocks,))],
         compiler_params=params(5),
@@ -269,7 +264,9 @@
 def gram_kernel(first, last, v0_ref, v1_ref, after_ref, out_ref):
     at = pl.ds(first, last - first)
     reads = (v0_ref.at[at], v1_ref.at[at])
-    out_ref[0], out_ref[1] = products_of(((0, 1), (1, 1)), reads, last - first, v0_ref.shape[1])
+    sums = products_of(((0, 0), (0, 1), (1, 1)), reads, last - first, v0_ref.shape[1])
+    for n, value in enumerate(sums):
+        out_ref[n] = value
 
 
 def gram_call(v0, v1, after, first, last):
@@ -279,7 +276,7 @@
         functools.partial(gram_kernel, first, last),
         in_specs=[vmem, vmem, pl.BlockSpec(memory_space=pltpu.HBM)],
         out_specs=vmem,
-        out_shape=jax.ShapeDtypeStruct((2, 8, 256), F32),
+        out_shape=jax.ShapeDtypeStruct((3, 8, 256), F32),
         compiler_params=params(2),
         cost_estimate=pl.CostEstimate(flops=4 * size, bytes_accessed=4 * size, transcendentals=0),
         name="gram",
@@ -390,7 +387,7 @@
     )(*parts, after)
 
 
-def products_kernel(scale, cuts, column_ref, h_ref, t0_ref, square_ref, *refs):
+def products_kernel(scale, cuts, column_ref, h_ref, t0_ref, *refs):
     out_ref = refs[-1]
     cots, tangents, grams = refs[:cuts], refs[cuts : 2 * cuts], refs[2 * cuts : -1]
     sources, rows, wide = cots[0].shape
@@ -410,9 +407,9 @@
         jnp.sum(c0),
         jnp.sum(c1),
         jnp.sum(weight * square) * (scale * scale),
-        jnp.sum(square_ref[...]),
         jnp.sum(sum(ref[0] for ref in grams)),
         jnp.sum(sum(ref[1] for ref in grams)),
+        jnp.sum(sum(ref[2] for ref in grams)),
     )
     lane = lax.broadcasted_iota(jnp.int32, out_ref.shape, 2)
     out = jnp.zeros(out_ref.shape, F32)
@@ -421,9 +418,9 @@
     out_ref[...] = out
 
 
-def products_call(column, hidden, t0, square, cots, tangents, grams, scale, devices):
+def products_call(column, hidden, t0, cots, tangents, grams, scale, devices):
     vmem = pl.BlockSpec(memory_space=pltpu.VMEM)
-    args = (hidden, t0, square, *cots, *tangents, *grams)
+    args = (hidden, t0, *cots, *tangents, *grams)
     return pl.pallas_call(
         functools.partial(products_kernel, scale, len(cots)),
         in_specs=[pl.BlockSpec(memory_space=pltpu.SMEM)] + [vmem] * len(args),
@@ -541,11 +538,11 @@
         got = [lax.psum(tangents[0], "slice")]
     shares = share_call(got, rho_row, line, (v1,))
     got = [shares[0]] + [swap(shares[j], "dp", j) for j in range(1, sources)]
-    v0, t0, hidden_t, square = other_call(hidden, basis, shares[0], v1, chunks, scale)
+    v0, t0, hidden_t = other_call(hidden, basis, shares[0], v1, chunks, scale)
     summed, rho_all = sum_call(got, rho_row, line, (v0, v1), hidden_t)
     got = [summed] + [swap(summed, "group", j) for j in range(1, E)]
     units = v0.shape[0]
-    cut = units // 4 * 3
+    cut = units * 5 // 8 // 32 * 32
     grams = [gram_call(v0, v1, rho_all, 0, cut)]
     cot = cotangent_call(got, placing, rho_all, sigma_row, kappa, (v0, v1), grams[0])
     cots = [cot] + [swap(cot, "dp", j) for j in range(1, sources)]
@@ -554,7 +551,7 @@
     cots = [cots] + ([swap(cots, "slice", j) for j in range(1, slices)] if split else [])
 
     devices = sources * E * slices
-    parts = products_call(column, hidden, t0, square, cots, tangents, grams, scale, devices)
+    parts = products_call(column, hidden, t0, cots, tangents, grams, scale, devices)
     parts = lax.all_to_all(parts, EVERY, 0, 0, tiled=True)
     new, hess = final_call(column, parts, hidden_t, cots, v0, v1, scale, entries)
     return new, hess.T

time: 78.6 us -> 75.3 us (0.958)
  Pallas kernels: 43.6 us -> 41.1 us
    pallas_call x1, Pallas kernels: 8.16 us -> 5.35 us  [other_call(): pl.pallas_call(functools.partial(other_kernel, scale), in_specs=[vmem, hb...]
  transfers between devices with their start and end apart: 14 -> 14, of which waited for: 6 -> 5; matrix products, arithmetic and copies ran while one was open for 0% -> 0% of each run, Pallas kernels for 29% -> 27%
where the time goes in v4:
time: 75.3 us; the launch traced here: 75.1 us
  Pallas kernels  41.1 us (55%)
  starting transfers between devices  16.6 us (22%)
  blocking collectives  11.2 us (15%)
  waiting for transfers between devices  5.32 us (7%)
  between operations  0.79 us (1%)
    ppermute x14, starting transfers between devices, swap(): return lax.ppermute(x, axis, [(i, i ^ distance) for i in range(size)])  16.6 us
    all_to_all x1, blocking collectives, body(): parts = lax.all_to_all(parts, EVERY, 0, 0, tiled=True)  11.2 us
    pallas_call x1, Pallas kernels, final_call(): pl.pallas_call(functools.partial(final_kernel, scale, entries, sources),...  10.2 us
    pallas_call x1, Pallas kernels, hidden_call(): pl.pallas_call(functools.partial(hidden_kernel, scale, sources, cuts), in...  9.17 us
    pallas_call x1, Pallas kernels, load_call(): pl.pallas_call(functools.partial(load_kernel, tok_dev), in_specs=[pl.Bloc...  8.93 us
    pallas_call x2, Pallas kernels, gram_call(): pl.pallas_call(functools.partial(gram_kernel, first, last), in_specs=[vme...  5.85 us
    pallas_call x1, Pallas kernels, other_call(): pl.pallas_call(functools.partial(other_kernel, scale), in_specs=[vmem, hb...  5.35 us
    ppermute x14, waiting for transfers between devices, swap(): return lax.ppermute(x, axis, [(i, i ^ distance) for i in range(size)])  5.32 us
  transfers between devices with their start and end apart: 14, of which 5 were waited for; matrix products, arithmetic and copies ran while one was open for 0% of the time, Pallas kernels for 27%

profile of v4, /device:TPU:0, one launch (start us, length us, event | category | flops | bytes accessed | tf_op | source)
XLA Modules:
  0.0 75.1 jit_solution(14657801526252801892)
XLA Ops:
  0.6 3.0 %collective-permute-start.1 = (bf16[16,6144]{1,0:T(8,128)(2,1)}, bf16[16,6144]{1,0:T(8,128)(2,1)S(1)}, u32[]{:S(2)}, u32[]{:S(2)}) collective-permute-start(bf16[16,6144]{1,0:T(8,128)(2,1)} %refs_0_.1), channel_id=1, source_target_pairs={{0,16},{8,24},{16,0},{24,8},{1,17},{9,25},{17,1},{25,9},{2,18},{10... | collective-permute-start | bytes 589832 | tf_op jit(solution)/shard_map/ppermute | solution.py:507
  3.7 1.5 %collective-permute-start = (bf16[16,6144]{1,0:T(8,128)(2,1)}, bf16[16,6144]{1,0:T(8,128)(2,1)S(1)}, u32[]{:S(2)}, u32[]{:S(2)}) collective-permute-start(bf16[16,6144]{1,0:T(8,128)(2,1)} %refs_0_.1), channel_id=1, source_target_pairs={{0,8},{8,0},{16,24},{24,16},{1,9},{9,1},{17,25},{25,17},{2,10},{10... | collective-permute-start | bytes 589832 | tf_op jit(solution)/shard_map/ppermute | solution.py:507
  5.2 0.1 collective-permute-start.2
  5.2 0.1 pad_add_fusion.ids_ref
  5.3 0.0 copy-start
  5.3 8.9 %load.1 = (bf16[6144,1024]{1,0:T(8,128)(2,1)S(1)}, bf16[6144,1024]{1,0:T(8,128)(2,1)S(1)}, bf16[4,40,64]{2,1,0:T(8,128)(2,1)S(1)}, f32[64,1]{1,0:T(8,128)S(1)}, ...) custom-call(s32[3]{0:T(128)S(1)} %pad_add_fusion.ids_ref, s32[2,64]{1,0:T(2,128)} %bitcast.10, f32[2,64]{1,0:T(2,128)} %bitcast.11, ...), custom_call_target="tpu_custom_call" | custom-call | bytes 50331648 | tf_op jit(solution)/shard_map/load/pallas_call | solution.py:98
  14.3 0.0 collective-permute-done.1.refs_2_
  14.3 0.0 collective-permute-done.refs_1_
  14.3 0.0 collective-permute-done.2.refs_3_
  14.3 0.0 copy-done
  14.3 9.2 %hidden.1 = (bf16[40,1024]{1,0:T(8,128)(2,1)S(1)}, bf16[1024,6144]{1,0:T(8,128)(2,1)S(1)}, f32[4,40,768]{2,1,0:T(8,128)S(1)}, bf16[4,40,768]{2,1,0:T(8,128)(2,1)S(1)}) custom-call(s32[8]{0:T(128)S(1)} %fusion.2.column_ref, bf16[16,6144]{1,0:T(8,128)(2,1)S(1)} %copy-done, bf16[16,6144]{1,0:T(8,128)(2,1)S(1)} %collective-permute-done.refs_1_, ...), custom_call_target="tpu_custom_call" | custom-call | flops 1509949440 | bytes 37748736 | tf_op jit(solution)/shard_map/hidden/pallas_call | solution.py:171
  23.5 0.1 collective-permute-start.3
  23.6 1.5 %collective-permute-done.3.refs_1_ = bf16[4,40,768]{2,1,0:T(8,128)(2,1)S(1)} collective-permute-done((bf16[4,40,768]{2,1,0:T(8,128)(2,1)S(1)}, bf16[4,40,768]{2,1,0:T(8,128)(2,1)S(1)}, u32[]{:S(2)}, u32[]{:S(2)}) %collective-permute-start.3) | collective-permute-done | bytes 245792 | tf_op jit(solution)/shard_map/ppermute | solution.py:507
  25.1 0.1 slice_sum.1
  25.1 2.0 %collective-permute-start.4 = (bf16[40,768]{1,0:T(8,128)(2,1)S(1)}, bf16[40,768]{1,0:T(8,128)(2,1)S(1)}, u32[]{:S(2)}, u32[]{:S(2)}) collective-permute-start(bf16[40,768]{1,0:T(8,128)(2,1)S(1)} %get-tuple-element.34), channel_id=1, source_target_pairs={{0,8},{8,0},{16,24},{24,16},{1,9},{9,1},{17,25},{25,17},{2,10},{10... | collective-permute-start | bytes 184328 | tf_op jit(solution)/shard_map/ppermute | solution.py:507
  27.1 1.5 %collective-permute-start.5 = (bf16[40,768]{1,0:T(8,128)(2,1)S(1)}, bf16[40,768]{1,0:T(8,128)(2,1)S(1)}, u32[]{:S(2)}, u32[]{:S(2)}) collective-permute-start(bf16[40,768]{1,0:T(8,128)(2,1)S(1)} %get-tuple-element.35), channel_id=1, source_target_pairs={{0,16},{8,24},{16,0},{24,8},{1,17},{9,25},{17,1},{25,9},{2,18},{10... | collective-permute-start | bytes 184328 | tf_op jit(solution)/shard_map/ppermute | solution.py:507
  28.6 0.0 collective-permute-start.6
  28.7 5.3 %other_tangent.1 = (bf16[1024,6144]{1,0:T(8,128)(2,1)S(1)}, bf16[8,40,768]{2,1,0:T(8,128)(2,1)S(1)}, bf16[1024,40]{1,0:T(8,128)(2,1)S(1)}) custom-call(bf16[40,1024]{1,0:T(8,128)(2,1)S(1)} %get-tuple-element.27.h_ref, bf16[2,1024,6144]{2,1,0:T(8,128)(2,1)} %v_hbm.1, f32[40,768]{1,0:T(8,128)S(1)} %get-tuple-element.32.after_ref.refs_0_, ...), custom_call_target="tpu_custom_call" | custom-call | flops 503316480 | bytes 12582912 | tf_op jit(solution)/shard_map/other_tangent/pallas_call | solution.py:246
  34.0 0.0 collective-permute-done.4.refs_1_
  34.0 0.0 collective-permute-done.5.refs_2_
  34.1 0.0 collective-permute-done.6.refs_3_
  34.1 4.1 %collective-permute-start.9 = (bf16[40,768]{1,0:T(8,128)(2,1)S(1)}, bf16[40,768]{1,0:T(8,128)(2,1)S(1)}, u32[]{:S(2)}, u32[]{:S(2)}) collective-permute-start(bf16[40,768]{1,0:T(8,128)(2,1)S(1)} %get-tuple-element.41.refs_0_), channel_id=1, source_target_pairs={{0,6},{2,4},{4,2},{6,0},{1,7},{3,5},{5,3},{7,1},{8,14},{10,12},{12... | collective-permute-start | bytes 184328 | tf_op jit(solution)/shard_map/ppermute | solution.py:507
  38.2 0.0 collective-permute-start.8
  38.2 0.6 collective-permute-start.7
  38.9 3.6 %gram.2.refs_6_.refs_4_ = f32[3,8,256]{2,1,0:T(8,128)S(1)} custom-call(bf16[1024,6144]{1,0:T(8,128)(2,1)S(1)} %get-tuple-element.37.refs_5_.v0_ref.refs_4_, bf16[1024,6144]{1,0:T(8,128)(2,1)S(1)} %get-tuple-element.31.refs_3_.held_ref.refs_6_.v1_ref.refs_5_, f32[4,128]{1,0:T(4,128)S(1)} %get-tuple-element.39.after_ref.rho_ref), custom_call_target="tpu_custom_call" | custom-call | flops 15728640 | bytes 15728640 | tf_op jit(solution)/shard_map/gram/pallas_call | solution.py:275
  42.5 0.0 collective-permute-done.9.refs_3_
  42.5 0.9 %collective-permute-done.8.refs_2_ = bf16[40,768]{1,0:T(8,128)(2,1)S(1)} collective-permute-done((bf16[40,768]{1,0:T(8,128)(2,1)S(1)}, bf16[40,768]{1,0:T(8,128)(2,1)S(1)}, u32[]{:S(2)}, u32[]{:S(2)}) %collective-permute-start.8) | collective-permute-done | bytes 61472 | tf_op jit(solution)/shard_map/ppermute | solution.py:507
  43.4 0.0 collective-permute-done.7.refs_1_
  43.4 0.5 cotangent.1.after_ref.refs_0_
  43.8 2.5 %collective-permute-start.12 = (bf16[40,768]{1,0:T(8,128)(2,1)S(1)}, bf16[40,768]{1,0:T(8,128)(2,1)S(1)}, u32[]{:S(2)}, u32[]{:S(2)}) collective-permute-start(bf16[40,768]{1,0:T(8,128)(2,1)S(1)} %cotangent.1.after_ref.refs_0_), channel_id=1, source_target_pairs={{0,24},{8,16},{16,8},{24,0},{1,25},{9,17},{17,9},{25,1},{2,26},{10... | collective-permute-start | bytes 184328 | tf_op jit(solution)/shard_map/ppermute | solution.py:507
  46.3 0.5 collective-permute-start.11
  46.8 0.5 collective-permute-start.10
  47.4 2.2 %gram.3.refs_4_.refs_5_ = f32[3,8,256]{2,1,0:T(8,128)S(1)} custom-call(bf16[1024,6144]{1,0:T(8,128)(2,1)S(1)} %get-tuple-element.37.refs_5_.v0_ref.refs_4_, bf16[1024,6144]{1,0:T(8,128)(2,1)S(1)} %get-tuple-element.31.refs_3_.held_ref.refs_6_.v1_ref.refs_5_, bf16[40,768]{1,0:T(8,128)(2,1)S(1)} %cotangent.1.after_ref.refs_0_), custom_call_target="tpu_custom_call" | custom-call | flops 9437184 | bytes 9437184 | tf_op jit(solution)/shard_map/gram/pallas_call | solution.py:275
  49.6 0.0 collective-permute-done.12.refs_3_
  49.6 0.9 %collective-permute-done.11.refs_2_ = bf16[40,768]{1,0:T(8,128)(2,1)S(1)} collective-permute-done((bf16[40,768]{1,0:T(8,128)(2,1)S(1)}, bf16[40,768]{1,0:T(8,128)(2,1)S(1)}, u32[]{:S(2)}, u32[]{:S(2)}) %collective-permute-start.11) | collective-permute-done | bytes 61472 | tf_op jit(solution)/shard_map/ppermute | solution.py:507
  50.5 0.5 collective-permute-done.10.refs_1_
  51.1 0.1 collective-permute-start.13
  51.2 1.5 %collective-permute-done.13.refs_1_ = bf16[4,40,768]{2,1,0:T(8,128)(2,1)S(1)} collective-permute-done((bf16[4,40,768]{2,1,0:T(8,128)(2,1)S(1)}, bf16[4,40,768]{2,1,0:T(8,128)(2,1)S(1)}, u32[]{:S(2)}, u32[]{:S(2)}) %collective-permute-start.13) | collective-permute-done | bytes 245792 | tf_op jit(solution)/shard_map/ppermute | solution.py:507
  52.7 1.1 %products.1 = f32[32,1,128]{2,1,0:T(1,128)S(1)} custom-call(s32[8]{0:T(128)S(1)} %fusion.2.column_ref, bf16[40,1024]{1,0:T(8,128)(2,1)S(1)} %get-tuple-element.27.h_ref, bf16[8,40,768]{2,1,0:T(8,128)(2,1)S(1)} %get-tuple-element.33.t0_ref, bf16[4,40,768]{2,1,0:T(8,128)(2,1)S(1)} %stack.13.refs_0_, bf16[4,40,768]{2,1,0:T(8,128)(2,1)S(1)} %collective-permute-done.13.refs_1_, ...), custom_call_target="tpu_custom_call" | custom-call | tf_op jit(solution)/shard_map/products/pallas_call | solution.py:424
  53.7 11.2 %all_to_all.5.parts_ref = f32[32,1,128]{2,1,0:T(1,128)S(1)} all-to-all(f32[32,1,128]{2,1,0:T(1,128)S(1)} %products.1), channel_id=1, replica_groups=mesh['dp'=4,'group'=4,'slice'=2] {'dp','group','slice'}, dimensions={0} | all-to-all | bytes 32768 | tf_op jit(solution)/shard_map/all_to_all | solution.py:555
  64.9 10.2 %residual.1 = (bf16[1024,6144]{1,0:T(8,128)(2,1)}, f32[1,3]{1,0:T(1,128)}) custom-call(s32[8]{0:T(128)S(1)} %fusion.2.column_ref, f32[32,1,128]{2,1,0:T(1,128)S(1)} %all_to_all.5.parts_ref, bf16[1024,40]{1,0:T(8,128)(2,1)S(1)} %get-tuple-element.38.refs_7_.ht_ref, bf16[1024,6144]{1,0:T(8,128)(2,1)S(1)} %get-tuple-element.37.refs_5_.v0_ref.refs_4_, ...), custom_call_target="tpu_custom_call" | custom-call | flops 503316480 | bytes 37748736 | tf_op jit(solution)/shard_map/residual/pallas_call | solution.py:475
  (3 shorter events, 0.1 us)
Async XLA Ops:
  0.6 13.6 %collective-permute-start.1 = (bf16[16,6144]{1,0:T(8,128)(2,1)}, bf16[16,6144]{1,0:T(8,128)(2,1)S(1)}, u32[]{:S(2)}, u32[]{:S(2)}) collective-permute-start(bf16[16,6144]{1,0:T(8,128)(2,1)} %refs_0_.1), channel_id=1, source_target_pairs={{0,16},{8,24},{16,0},{24,8},{1,17},{9,25},{17,1},{25,9},{2,18},{10... | collective-permute-start | bytes 589832 | tf_op jit(solution)/shard_map/ppermute | solution.py:507
  3.7 10.6 %collective-permute-start = (bf16[16,6144]{1,0:T(8,128)(2,1)}, bf16[16,6144]{1,0:T(8,128)(2,1)S(1)}, u32[]{:S(2)}, u32[]{:S(2)}) collective-permute-start(bf16[16,6144]{1,0:T(8,128)(2,1)} %refs_0_.1), channel_id=1, source_target_pairs={{0,8},{8,0},{16,24},{24,16},{1,9},{9,1},{17,25},{25,17},{2,10},{10... | collective-permute-start | bytes 589832 | tf_op jit(solution)/shard_map/ppermute | solution.py:507
  5.2 9.1 %collective-permute-start.2 = (bf16[16,6144]{1,0:T(8,128)(2,1)}, bf16[16,6144]{1,0:T(8,128)(2,1)S(1)}, u32[]{:S(2)}, u32[]{:S(2)}) collective-permute-start(bf16[16,6144]{1,0:T(8,128)(2,1)} %refs_0_.1), channel_id=1, source_target_pairs={{0,24},{8,16},{16,8},{24,0},{1,25},{9,17},{17,9},{25,1},{2,26},{10... | collective-permute-start | bytes 589832 | tf_op jit(solution)/shard_map/ppermute | solution.py:507
  5.3 9.0 %copy-start = (bf16[16,6144]{1,0:T(8,128)(2,1)S(1)}, bf16[16,6144]{1,0:T(8,128)(2,1)}, u32[]{:S(2)}) copy-start(bf16[16,6144]{1,0:T(8,128)(2,1)} %refs_0_.1) | copy-start | bytes 589828
  23.5 1.6 %collective-permute-start.3 = (bf16[4,40,768]{2,1,0:T(8,128)(2,1)S(1)}, bf16[4,40,768]{2,1,0:T(8,128)(2,1)S(1)}, u32[]{:S(2)}, u32[]{:S(2)}) collective-permute-start(bf16[4,40,768]{2,1,0:T(8,128)(2,1)S(1)} %get-tuple-element.29.refs_3_), channel_id=1, source_target_pairs={{0,1},{1,0},{2,3},{3,2},{4,5},{5,4},{6,7},{7,6},{8,9},{9,8},{10,11... | collective-permute-start | bytes 737288 | tf_op jit(solution)/shard_map/ppermute | solution.py:507
  25.1 8.9 %collective-permute-start.4 = (bf16[40,768]{1,0:T(8,128)(2,1)S(1)}, bf16[40,768]{1,0:T(8,128)(2,1)S(1)}, u32[]{:S(2)}, u32[]{:S(2)}) collective-permute-start(bf16[40,768]{1,0:T(8,128)(2,1)S(1)} %get-tuple-element.34), channel_id=1, source_target_pairs={{0,8},{8,0},{16,24},{24,16},{1,9},{9,1},{17,25},{25,17},{2,10},{10... | collective-permute-start | bytes 184328 | tf_op jit(solution)/shard_map/ppermute | solution.py:507
  27.1 6.9 %collective-permute-start.5 = (bf16[40,768]{1,0:T(8,128)(2,1)S(1)}, bf16[40,768]{1,0:T(8,128)(2,1)S(1)}, u32[]{:S(2)}, u32[]{:S(2)}) collective-permute-start(bf16[40,768]{1,0:T(8,128)(2,1)S(1)} %get-tuple-element.35), channel_id=1, source_target_pairs={{0,16},{8,24},{16,0},{24,8},{1,17},{9,25},{17,1},{25,9},{2,18},{10... | collective-permute-start | bytes 184328 | tf_op jit(solution)/shard_map/ppermute | solution.py:507
  28.6 5.4 %collective-permute-start.6 = (bf16[40,768]{1,0:T(8,128)(2,1)S(1)}, bf16[40,768]{1,0:T(8,128)(2,1)S(1)}, u32[]{:S(2)}, u32[]{:S(2)}) collective-permute-start(bf16[40,768]{1,0:T(8,128)(2,1)S(1)} %get-tuple-element.36), channel_id=1, source_target_pairs={{0,24},{8,16},{16,8},{24,0},{1,25},{9,17},{17,9},{25,1},{2,26},{10... | collective-permute-start | bytes 184328 | tf_op jit(solution)/shard_map/ppermute | solution.py:507
  34.1 8.4 %collective-permute-start.9 = (bf16[40,768]{1,0:T(8,128)(2,1)S(1)}, bf16[40,768]{1,0:T(8,128)(2,1)S(1)}, u32[]{:S(2)}, u32[]{:S(2)}) collective-permute-start(bf16[40,768]{1,0:T(8,128)(2,1)S(1)} %get-tuple-element.41.refs_0_), channel_id=1, source_target_pairs={{0,6},{2,4},{4,2},{6,0},{1,7},{3,5},{5,3},{7,1},{8,14},{10,12},{12... | collective-permute-start | bytes 184328 | tf_op jit(solution)/shard_map/ppermute | solution.py:507
  38.2 5.1 %collective-permute-start.8 = (bf16[40,768]{1,0:T(8,128)(2,1)S(1)}, bf16[40,768]{1,0:T(8,128)(2,1)S(1)}, u32[]{:S(2)}, u32[]{:S(2)}) collective-permute-start(bf16[40,768]{1,0:T(8,128)(2,1)S(1)} %get-tuple-element.41.refs_0_), channel_id=1, source_target_pairs={{0,4},{2,6},{4,0},{6,2},{1,5},{3,7},{5,1},{7,3},{8,12},{10,14},{12... | collective-permute-start | bytes 184328 | tf_op jit(solution)/shard_map/ppermute | solution.py:507
  38.2 5.1 %collective-permute-start.7 = (bf16[40,768]{1,0:T(8,128)(2,1)S(1)}, bf16[40,768]{1,0:T(8,128)(2,1)S(1)}, u32[]{:S(2)}, u32[]{:S(2)}) collective-permute-start(bf16[40,768]{1,0:T(8,128)(2,1)S(1)} %get-tuple-element.41.refs_0_), channel_id=1, source_target_pairs={{0,2},{2,0},{4,6},{6,4},{1,3},{3,1},{5,7},{7,5},{8,10},{10,8},{12,... | collective-permute-start | bytes 184328 | tf_op jit(solution)/shard_map/ppermute | solution.py:507
  43.8 5.8 %collective-permute-start.12 = (bf16[40,768]{1,0:T(8,128)(2,1)S(1)}, bf16[40,768]{1,0:T(8,128)(2,1)S(1)}, u32[]{:S(2)}, u32[]{:S(2)}) collective-permute-start(bf16[40,768]{1,0:T(8,128)(2,1)S(1)} %cotangent.1.after_ref.refs_0_), channel_id=1, source_target_pairs={{0,24},{8,16},{16,8},{24,0},{1,25},{9,17},{17,9},{25,1},{2,26},{10... | collective-permute-start | bytes 184328 | tf_op jit(solution)/shard_map/ppermute | solution.py:507
  46.3 4.2 %collective-permute-start.11 = (bf16[40,768]{1,0:T(8,128)(2,1)S(1)}, bf16[40,768]{1,0:T(8,128)(2,1)S(1)}, u32[]{:S(2)}, u32[]{:S(2)}) collective-permute-start(bf16[40,768]{1,0:T(8,128)(2,1)S(1)} %cotangent.1.after_ref.refs_0_), channel_id=1, source_target_pairs={{0,16},{8,24},{16,0},{24,8},{1,17},{9,25},{17,1},{25,9},{2,18},{10... | collective-permute-start | bytes 184328 | tf_op jit(solution)/shard_map/ppermute | solution.py:507
  46.8 4.2 %collective-permute-start.10 = (bf16[40,768]{1,0:T(8,128)(2,1)S(1)}, bf16[40,768]{1,0:T(8,128)(2,1)S(1)}, u32[]{:S(2)}, u32[]{:S(2)}) collective-permute-start(bf16[40,768]{1,0:T(8,128)(2,1)S(1)} %cotangent.1.after_ref.refs_0_), channel_id=1, source_target_pairs={{0,8},{8,0},{16,24},{24,16},{1,9},{9,1},{17,25},{25,17},{2,10},{10... | collective-permute-start | bytes 184328 | tf_op jit(solution)/shard_map/ppermute | solution.py:507
  51.1 1.6 %collective-permute-start.13 = (bf16[4,40,768]{2,1,0:T(8,128)(2,1)S(1)}, bf16[4,40,768]{2,1,0:T(8,128)(2,1)S(1)}, u32[]{:S(2)}, u32[]{:S(2)}) collective-permute-start(bf16[4,40,768]{2,1,0:T(8,128)(2,1)S(1)} %stack.13.refs_0_), channel_id=1, source_target_pairs={{0,1},{1,0},{2,3},{3,2},{4,5},{5,4},{6,7},{7,6},{8,9},{9,8},{10,11... | collective-permute-start | bytes 737288 | tf_op jit(solution)/shard_map/ppermute | solution.py:507
